TPU v7x, 32 devices: a whole 2x2x4 slice. The times are simulated.
32 devices in a mesh: section: 4 (over y, core), seq: 8 (over z, x).
Axes of the slice: x: 2, y: 2, z: 4, core: 2. Of those that a mesh axis runs over, the one named last changes fastest.
Arguments:
- base_ids: int32 [2, 1024], P(None, 'seq'), may hold values from 0 to 3
- stem_weight: bfloat16 [15, 4, 768], replicated, may hold values from -1.5 to 1.5
- conv_weight: bfloat16 [4, 5, 768, 768], P('section'), may hold values from -0.09375 to 0.09375
- block_gain: float32 [4, 768], P('section'), may hold values from 0.1 to 1.9
- cotangent: bfloat16 [2, 1024, 768], P(None, 'seq'), may hold values from -0.29882812 to 0.29882812
Outputs:
- conv_grad: bfloat16 [4, 5, 768, 768], P('section', None, 'seq')
- gain_grad: float32 [4, 768], P('section', 'seq')
All inputs are finite; a program needn't handle non-finite values.
Results may differ from a plain program's by a relative error of at most 0.035.
Values may be sent and summed in bfloat16 or wider, within the bound.
A program may use at most 128 MiB of HBM per device.

v0:
```python
import jax
import jax.numpy as jnp
from jax import lax
from jax.sharding import PartitionSpec as P

KERNEL = 5
STEM_K = 15
BASES = 4


def padded_2(array, sides, width):
    for axis, dim in sides:
        size, length = (lax.axis_size(axis), array.shape[dim])
        up = [(i, (i + 1) % size) for i in range(size - 1)]
        down = [(j, i) for i, j in up]
        last = lax.slice_in_dim(array, length - width, length, axis=dim)
        initial = lax.slice_in_dim(array, 0, width, axis=dim)
        before = lax.ppermute(last, axis, up)
        after = lax.ppermute(initial, axis, down)
        array = jnp.concatenate([before, array, after], axis=dim)
    return array


def passed_along(block, axis, distance):
    devices = range(lax.axis_size(axis))
    route = [(i - distance, i) for i in devices if i - distance in devices]
    return lax.ppermute(block, axis, route)


def activate(block_sum, gain_row):
    scale = lax.rsqrt(jnp.mean(block_sum * block_sum, axis=-1, keepdims=True) + 1e-06)
    return jax.nn.gelu(block_sum * scale * gain_row)


def mirror(payload):
    section_count = lax.axis_size("section")
    spread = lax.all_to_all(payload, "section", split_axis=0, concat_axis=0, tiled=True)
    flipped = spread.reshape(section_count, -1, payload.shape[1])[::-1].reshape(payload.shape)
    moved = lax.all_to_all(flipped, "section", split_axis=0, concat_axis=0, tiled=True)
    return moved


def put_slot(buffer, value, slot_index, accepted):
    previous = lax.dynamic_index_in_dim(buffer, slot_index, 0, keepdims=False)
    return lax.dynamic_update_index_in_dim(
        buffer, jnp.where(accepted, value, previous), slot_index, 0
    )


def shards(base_ids, stem_weight, conv_weight, block_gain, cotangent):
    section_count = lax.axis_size("section")
    my_section = lax.axis_index("section")
    half_count = section_count // 2
    micro_count, row_count, channels = cotangent.shape
    conv_reach = (KERNEL - 1) // 2
    stem_reach = (STEM_K - 1) // 2
    filters = conv_weight[0]
    gain_row = block_gain[0]
    is_first = my_section == 0
    is_last = my_section == section_count - 1
    decoder = my_section >= half_count
    encoder = my_section < half_count
    padded_ids = padded_2(base_ids + 1, (("seq", 1),), stem_reach)
    letters = jnp.arange(1, BASES + 1, dtype=jnp.int32)
    matches = [
        padded_ids[:, offset : offset + row_count, None] == letters for offset in range(STEM_K)
    ]
    onehot = jnp.concatenate(matches, axis=2).astype(jnp.bfloat16)
    stem_out = jnp.einsum(
        "ohs,sn->ohn",
        onehot,
        stem_weight.reshape(STEM_K * BASES, channels),
        preferred_element_type=jnp.float32,
    ).astype(jnp.bfloat16)
    empty_tile = jnp.zeros((row_count, channels), jnp.bfloat16)

    def conv_out(block_sum, padded):
        summed = block_sum
        for offset in range(KERNEL):
            summed = summed + jnp.dot(
                padded[offset : offset + row_count],
                filters[offset],
                preferred_element_type=jnp.float32,
            )
        return summed.astype(jnp.bfloat16)

    def forward_tick(tick, state_tuple, sending):
        inflow, skip_store, stored_sums, stored_rows = state_tuple
        micro_slot = tick - my_section
        active = (micro_slot >= 0) & (micro_slot < micro_count)
        slot_index = jnp.clip(micro_slot, 0, micro_count - 1)
        from_stem = lax.dynamic_index_in_dim(stem_out, slot_index, 0, keepdims=False)
        block_in = jnp.where(is_first, from_stem, inflow)
        joined = lax.dynamic_index_in_dim(skip_store, slot_index, 0, keepdims=False)
        block_sum = block_in.astype(jnp.float32) + jnp.where(
            decoder, joined.astype(jnp.float32), 0.0
        )
        activated = activate(block_sum, gain_row).astype(jnp.bfloat16)
        padded = padded_2(activated, (("seq", 0),), conv_reach)
        block_out = lax.cond(
            active & jnp.logical_not(is_last),
            lambda: conv_out(block_sum, padded),
            lambda: empty_tile,
        )
        stored_sums = put_slot(stored_sums, block_sum, slot_index, active)
        stored_rows = put_slot(stored_rows, padded, slot_index, active)
        if sending:
            arrived = mirror(block_out)
            mirror_slot = tick - (section_count - 1 - my_section)
            accepted = decoder & (mirror_slot >= 0) & (mirror_slot < micro_count)
            mirror_index = jnp.clip(mirror_slot, 0, micro_count - 1)
            skip_store = put_slot(skip_store, arrived, mirror_index, accepted)
        inflow = passed_along(block_out, "section", 1)
        return (inflow, skip_store, stored_sums, stored_rows)

    rows_start = jnp.zeros((micro_count, row_count + 2 * conv_reach, channels), jnp.bfloat16)
    split_tick = half_count + micro_count - 1
    tick_count = section_count + micro_count - 1
    state_tuple = (
        empty_tile,
        jnp.zeros((micro_count, row_count, channels), jnp.bfloat16),
        jnp.zeros((micro_count, row_count, channels), jnp.float32),
        rows_start,
    )
    state_tuple = lax.fori_loop(
        0, split_tick, lambda tick, held: forward_tick(tick, held, True), state_tuple
    )
    state_tuple = lax.fori_loop(
        split_tick, tick_count, lambda tick, held: forward_tick(tick, held, False), state_tuple
    )
    unused_flow, unused_skips, stored_sums, stored_rows = state_tuple

    def backward_tick(tick, state_tuple, sending):
        grad_flow, skip_grads, kernel_sum, gain_sum = state_tuple
        micro_slot = tick - (section_count - 1 - my_section)
        active = (micro_slot >= 0) & (micro_slot < micro_count)
        slot_index = jnp.clip(micro_slot, 0, micro_count - 1)
        from_cot = lax.dynamic_index_in_dim(cotangent, slot_index, 0, keepdims=False)
        from_next = jnp.where(is_last, from_cot, grad_flow).astype(jnp.float32)
        from_skip = lax.dynamic_index_in_dim(skip_grads, slot_index, 0, keepdims=False)
        grad_out = (from_next + jnp.where(encoder, from_skip.astype(jnp.float32), 0.0)).astype(
            jnp.bfloat16
        )
        block_sum = lax.dynamic_index_in_dim(stored_sums, slot_index, 0, keepdims=False)
        padded = lax.dynamic_index_in_dim(stored_rows, slot_index, 0, keepdims=False)
        grad_padded = padded_2(grad_out, (("seq", 0),), conv_reach)

        def backward_block():
            kernel_terms = jnp.stack(
                [
                    jnp.einsum(
                        "rc,rd->cd",
                        padded[offset : offset + row_count],
                        grad_out,
                        preferred_element_type=jnp.float32,
                    )
                    for offset in range(KERNEL)
                ]
            )
            grad_act = jnp.zeros((row_count, channels), jnp.float32)
            for offset in range(KERNEL):
                start = 2 * conv_reach - offset
                grad_act = grad_act + jnp.einsum(
                    "rd,cd->rc",
                    grad_padded[start : start + row_count],
                    filters[offset],
                    preferred_element_type=jnp.float32,
                )
            unused_out, pullback = jax.vjp(activate, block_sum, gain_row)
            grad_norm_in, grad_gain = pullback(grad_act)
            grad_in = (grad_out.astype(jnp.float32) + grad_norm_in).astype(jnp.bfloat16)
            return (kernel_sum + kernel_terms, gain_sum + grad_gain, grad_in)

        def unused_block():
            return (kernel_sum, gain_sum, empty_tile)

        kernel_sum, gain_sum, grad_in = lax.cond(active, backward_block, unused_block)
        if sending:
            arrived = mirror(grad_in)
            return_slot = tick - my_section
            accepted = encoder & (return_slot >= 0) & (return_slot < micro_count)
            return_index = jnp.clip(return_slot, 0, micro_count - 1)
            skip_grads = put_slot(skip_grads, arrived, return_index, accepted)
        grad_flow = passed_along(grad_in, "section", -1)
        return (grad_flow, skip_grads, kernel_sum, gain_sum)

    state_tuple = (
        empty_tile,
        jnp.zeros((micro_count, row_count, channels), jnp.bfloat16),
        jnp.zeros((KERNEL, channels, channels), jnp.float32),
        jnp.zeros((channels,), jnp.float32),
    )
    state_tuple = lax.fori_loop(
        0, split_tick, lambda tick, held: backward_tick(tick, held, True), state_tuple
    )
    state_tuple = lax.fori_loop(
        split_tick, tick_count, lambda tick, held: backward_tick(tick, held, False), state_tuple
    )
    unused_flow, unused_grads, kernel_sum, gain_sum = state_tuple
    kernel_part, gain_part = (
        lax.psum_scatter(
            kernel_sum.astype(jnp.bfloat16), "seq", scatter_dimension=1, tiled=True
        ).astype(jnp.float32),
        lax.psum_scatter(
            gain_sum.astype(jnp.bfloat16), "seq", scatter_dimension=0, tiled=True
        ).astype(jnp.float32),
    )
    return (kernel_part.astype(jnp.bfloat16)[None], gain_part[None])


def solution(mesh):
    placed = (
        P(None, "seq"),
        P(),
        P("section", None, None, None),
        P("section", None),
        P(None, "seq", None),
    )
    return jax.shard_map(
        shards,
        mesh=mesh,
        in_specs=placed,
        out_specs=(P("section", None, "seq", None), P("section", "seq")),
        check_vma=False,
    )
```

profile of v0, /device:TPU:0, one launch (start us, length us, event | category | flops | bytes accessed | tf_op | source)
XLA Modules:
  0.0 543.1 jit_solution(3439244842130138860)
XLA Ops:
  9.3 5.5 %collective-permute-start.12 = (s32[2,7]{1,0:T(2,128)S(1)}, s32[2,7]{1,0:T(2,128)S(1)}, u32[]{:S(2)}, u32[]{:S(2)}) collective-permute-start(s32[2,7]{1,0:T(2,128)S(1)} %get-tuple-element.1504), channel_id=1, source_target_pairs={{0,1},{1,2},{2,3},{3,4},{4,5},{5,6},{6,7},{8,9},{9,10},{10,11},{11... | collective-permute-start | bytes 176 | tf_op jit(solution)/shard_map/ppermute | solution.py:18
  16.9 106.7 %while.79 = (s32[]{:T(128)}, bf16[128,768]{1,0:T(8,128)(2,1)S(1)}, bf16[2,128,768]{2,1,0:T(8,128)(2,1)S(1)}, f32[2,128,768]{2,1,0:T(8,128)S(1)}, bf16[2,132,768]...) while((s32[]{:T(128)}, bf16[128,768]{1,0:T(8,128)(2,1)S(1)}, ...), condition=%wide.region_4.5_spmd, body=%wide.region_0.4_spmd.sunk | while | flops 759929984 | bytes 18576368 | solution.py:125
  19.5 5.4 %collective-permute-start.1 = (bf16[2,768]{1,0:T(2,128)(2,1)S(1)}, bf16[2,768]{1,0:T(2,128)(2,1)S(1)}, u32[]{:S(2)}, u32[]{:S(2)}) collective-permute-start(bf16[2,768]{1,0:T(2,128)(2,1)S(1)} %get-tuple-element.1817), channel_id=1, source_target_pairs={{0,1},{1,2},{2,3},{3,4},{4,5},{5,6},{6,7},{8,9},{9,10},{10,11},{11... | collective-permute-start | bytes 9224 | tf_op jit(solution)/shard_map/while/body/eval_jaxpr/ppermute | solution.py:18
  26.3 8.1 %conditional.8 = (bf16[128,768]{1,0:T(8,128)(2,1)S(1)}) conditional(s32[]{:T(128)} %convert_element_type.229, () %tuple.213, (bf16[132,768]{1,0:T(8,128)(2,1)S(1)}, bf16[5,768,768]{2,1,0:T(8,128)(2,1)}, f32[128,768]{1,0:T(8,128)S(1)}, bf16[128,768]{1,0:T(8,128)(2,1)S(1)}) %tuple.214), branch_computations={%region_2.2_spmd, %region_3.3_spmd} | conditional | flops 755564544 | bytes 10616840 | solution.py:100
  34.3 7.7 %all_to_all.66 = bf16[4,32,768]{2,1,0:T(8,128)(2,1)S(1)} all-to-all(bf16[4,32,768]{2,1,0:T(8,128)(2,1)S(1)} %bitcast.280), channel_id=1, replica_groups=mesh['section'=4,'seq'=8] {'section'}, dimensions={0} | all-to-all | bytes 393216 | tf_op jit(solution)/shard_map/while/body/eval_jaxpr/all_to_all | solution.py:37
  42.7 3.4 all-to-all-start.1
  46.4 2.4 collective-permute-start.2
  48.8 2.6 all-to-all-done.1
  54.0 5.7 %collective-permute-start.1 = (bf16[2,768]{1,0:T(2,128)(2,1)S(1)}, bf16[2,768]{1,0:T(2,128)(2,1)S(1)}, u32[]{:S(2)}, u32[]{:S(2)}) collective-permute-start(bf16[2,768]{1,0:T(2,128)(2,1)S(1)} %get-tuple-element.1817), channel_id=1, source_target_pairs={{0,1},{1,2},{2,3},{3,4},{4,5},{5,6},{6,7},{8,9},{9,10},{10,11},{11... | collective-permute-start | bytes 9224 | tf_op jit(solution)/shard_map/while/body/eval_jaxpr/ppermute | solution.py:18
  61.1 8.1 %conditional.8 = (bf16[128,768]{1,0:T(8,128)(2,1)S(1)}) conditional(s32[]{:T(128)} %convert_element_type.229, () %tuple.213, (bf16[132,768]{1,0:T(8,128)(2,1)S(1)}, bf16[5,768,768]{2,1,0:T(8,128)(2,1)}, f32[128,768]{1,0:T(8,128)S(1)}, bf16[128,768]{1,0:T(8,128)(2,1)S(1)}) %tuple.214), branch_computations={%region_2.2_spmd, %region_3.3_spmd} | conditional | flops 755564544 | bytes 10616840 | solution.py:100
  69.2 7.7 %all_to_all.66 = bf16[4,32,768]{2,1,0:T(8,128)(2,1)S(1)} all-to-all(bf16[4,32,768]{2,1,0:T(8,128)(2,1)S(1)} %bitcast.280), channel_id=1, replica_groups=mesh['section'=4,'seq'=8] {'section'}, dimensions={0} | all-to-all | bytes 393216 | tf_op jit(solution)/shard_map/while/body/eval_jaxpr/all_to_all | solution.py:37
  77.6 3.4 all-to-all-start.1
  81.2 2.4 collective-permute-start.2
  83.7 2.6 all-to-all-done.1
  88.9 5.7 %collective-permute-start.1 = (bf16[2,768]{1,0:T(2,128)(2,1)S(1)}, bf16[2,768]{1,0:T(2,128)(2,1)S(1)}, u32[]{:S(2)}, u32[]{:S(2)}) collective-permute-start(bf16[2,768]{1,0:T(2,128)(2,1)S(1)} %get-tuple-element.1817), channel_id=1, source_target_pairs={{0,1},{1,2},{2,3},{3,4},{4,5},{5,6},{6,7},{8,9},{9,10},{10,11},{11... | collective-permute-start | bytes 9224 | tf_op jit(solution)/shard_map/while/body/eval_jaxpr/ppermute | solution.py:18
  96.0 18.2 %all_to_all.66 = bf16[4,32,768]{2,1,0:T(8,128)(2,1)S(1)} all-to-all(bf16[4,32,768]{2,1,0:T(8,128)(2,1)S(1)} %bitcast.280), channel_id=1, replica_groups=mesh['section'=4,'seq'=8] {'section'}, dimensions={0} | all-to-all | bytes 393216 | tf_op jit(solution)/shard_map/while/body/eval_jaxpr/all_to_all | solution.py:37
  114.9 3.4 all-to-all-start.1
  118.5 2.4 collective-permute-start.2
  121.0 2.6 all-to-all-done.1
  123.7 37.9 %while.80 = (s32[]{:T(128)}, bf16[128,768]{1,0:T(8,128)(2,1)S(1)}, f32[2,128,768]{2,1,0:T(8,128)S(1)}, bf16[2,132,768]{2,1,0:T(8,128)(2,1)S(1)}, s32[]{:T(128)},...) while((s32[]{:T(128)}, bf16[128,768]{1,0:T(8,128)(2,1)S(1)}, ...), condition=%wide.region_9.10_spmd, body=%wide.region_5.9_spmd.sunk | while | flops 759831680 | bytes 16610206 | solution.py:128
  126.2 5.7 %collective-permute-start.4 = (bf16[2,768]{1,0:T(2,128)(2,1)S(1)}, bf16[2,768]{1,0:T(2,128)(2,1)S(1)}, u32[]{:S(2)}, u32[]{:S(2)}) collective-permute-start(bf16[2,768]{1,0:T(2,128)(2,1)S(1)} %get-tuple-element.1833), channel_id=1, source_target_pairs={{0,1},{1,2},{2,3},{3,4},{4,5},{5,6},{6,7},{8,9},{9,10},{10,11},{11... | collective-permute-start | bytes 9224 | tf_op jit(solution)/shard_map/while/body/eval_jaxpr/ppermute | solution.py:18
  133.4 2.5 collective-permute-start.5
  139.4 5.7 %collective-permute-start.4 = (bf16[2,768]{1,0:T(2,128)(2,1)S(1)}, bf16[2,768]{1,0:T(2,128)(2,1)S(1)}, u32[]{:S(2)}, u32[]{:S(2)}) collective-permute-start(bf16[2,768]{1,0:T(2,128)(2,1)S(1)} %get-tuple-element.1833), channel_id=1, source_target_pairs={{0,1},{1,2},{2,3},{3,4},{4,5},{5,6},{6,7},{8,9},{9,10},{10,11},{11... | collective-permute-start | bytes 9224 | tf_op jit(solution)/shard_map/while/body/eval_jaxpr/ppermute | solution.py:18
  146.6 14.0 %collective-permute-start.5 = (bf16[128,768]{1,0:T(8,128)(2,1)S(1)}, bf16[128,768]{1,0:T(8,128)(2,1)S(1)}, u32[]{:S(2)}, u32[]{:S(2)}) collective-permute-start(bf16[128,768]{1,0:T(8,128)(2,1)S(1)} %get-tuple-element.2089), channel_id=1, source_target_pairs={{0,8},{8,16},{16,24},{1,9},{9,17},{17,25},{2,10},{10,18},{18,26},{... | collective-permute-start | bytes 589832 | tf_op jit(solution)/shard_map/while/body/eval_jaxpr/ppermute | solution.py:27
  161.6 5.4 broadcast_in_dim.154
  167.0 163.2 %while.81 = (s32[]{:T(128)}, bf16[128,768]{1,0:T(8,128)(2,1)S(1)}, bf16[2,128,768]{2,1,0:T(8,128)(2,1)S(1)}, f32[5,768,768]{2,1,0:T(8,128)}, f32[768]{0:T(1024)S...) while((s32[]{:T(128)}, bf16[128,768]{1,0:T(8,128)(2,1)S(1)}, ...), condition=%wide.region_16.17_spmd, body=%wide.region_10.16_spmd.sunk | while | flops 1518127872 | bytes 83248296 | solution.py:193
  168.5 5.7 %collective-permute-start.7 = (bf16[2,768]{1,0:T(2,128)(2,1)S(1)}, bf16[2,768]{1,0:T(2,128)(2,1)S(1)}, u32[]{:S(2)}, u32[]{:S(2)}) collective-permute-start(bf16[2,768]{1,0:T(2,128)(2,1)S(1)} %get-tuple-element.1850), channel_id=1, source_target_pairs={{0,1},{1,2},{2,3},{3,4},{4,5},{5,6},{6,7},{8,9},{9,10},{10,11},{11... | collective-permute-start | bytes 9224 | tf_op jit(solution)/shard_map/while/body/eval_jaxpr/ppermute | solution.py:18
  175.6 36.9 %all_to_all.67 = bf16[4,32,768]{2,1,0:T(8,128)(2,1)S(1)} all-to-all(bf16[4,32,768]{2,1,0:T(8,128)(2,1)S(1)} %bitcast.279), channel_id=1, replica_groups=mesh['section'=4,'seq'=8] {'section'}, dimensions={0} | all-to-all | bytes 393216 | tf_op jit(solution)/shard_map/while/body/eval_jaxpr/all_to_all | solution.py:37
  213.2 3.4 all-to-all-start.3
  217.9 4.0 all-to-all-done.3
  223.4 5.7 %collective-permute-start.7 = (bf16[2,768]{1,0:T(2,128)(2,1)S(1)}, bf16[2,768]{1,0:T(2,128)(2,1)S(1)}, u32[]{:S(2)}, u32[]{:S(2)}) collective-permute-start(bf16[2,768]{1,0:T(2,128)(2,1)S(1)} %get-tuple-element.1850), channel_id=1, source_target_pairs={{0,1},{1,2},{2,3},{3,4},{4,5},{5,6},{6,7},{8,9},{9,10},{10,11},{11... | collective-permute-start | bytes 9224 | tf_op jit(solution)/shard_map/while/body/eval_jaxpr/ppermute | solution.py:18
  230.5 36.3 %all_to_all.67 = bf16[4,32,768]{2,1,0:T(8,128)(2,1)S(1)} all-to-all(bf16[4,32,768]{2,1,0:T(8,128)(2,1)S(1)} %bitcast.279), channel_id=1, replica_groups=mesh['section'=4,'seq'=8] {'section'}, dimensions={0} | all-to-all | bytes 393216 | tf_op jit(solution)/shard_map/while/body/eval_jaxpr/all_to_all | solution.py:37
  267.5 3.4 all-to-all-start.3
  272.2 4.0 all-to-all-done.3
  277.7 5.4 %collective-permute-start.7 = (bf16[2,768]{1,0:T(2,128)(2,1)S(1)}, bf16[2,768]{1,0:T(2,128)(2,1)S(1)}, u32[]{:S(2)}, u32[]{:S(2)}) collective-permute-start(bf16[2,768]{1,0:T(2,128)(2,1)S(1)} %get-tuple-element.1850), channel_id=1, source_target_pairs={{0,1},{1,2},{2,3},{3,4},{4,5},{5,6},{6,7},{8,9},{9,10},{10,11},{11... | collective-permute-start | bytes 9224 | tf_op jit(solution)/shard_map/while/body/eval_jaxpr/ppermute | solution.py:18
  284.5 36.3 %all_to_all.67 = bf16[4,32,768]{2,1,0:T(8,128)(2,1)S(1)} all-to-all(bf16[4,32,768]{2,1,0:T(8,128)(2,1)S(1)} %bitcast.279), channel_id=1, replica_groups=mesh['section'=4,'seq'=8] {'section'}, dimensions={0} | all-to-all | bytes 393216 | tf_op jit(solution)/shard_map/while/body/eval_jaxpr/all_to_all | solution.py:37
  321.5 3.4 all-to-all-start.3
  326.2 4.0 all-to-all-done.3
  330.3 85.6 %while.82 = (s32[]{:T(128)}, bf16[128,768]{1,0:T(8,128)(2,1)S(1)}, f32[5,768,768]{2,1,0:T(8,128)}, f32[768]{0:T(1024)S(1)}, s32[]{:T(128)}, /*index=5*/pred[]{:T...) while((s32[]{:T(128)}, bf16[128,768]{1,0:T(8,128)(2,1)S(1)}, ...), condition=%wide.region_23.24_spmd, body=%wide.region_17.23_spmd.sunk | while | flops 1518029568 | bytes 81282136 | solution.py:196
  330.6 5.1 collective-permute-start.10
  337.0 5.3 collective-permute-done.9
  342.4 28.2 %conditional.11 = (f32[5,768,768]{2,1,0:T(8,128)}, f32[768]{0:T(1024)S(1)}, bf16[128,768]{1,0:T(8,128)(2,1)S(1)}) conditional(s32[]{:T(128)} %convert_element_type.240, (f32[5,768,768]{2,1,0:T(8,128)}, f32[768]{0:T(1024)S(1)}) %tuple.226, (bf16[2,132,768]{2,1,0:T(8,128)(2,1)S(1)}, s32[]{:T(128)}, bf16[128,768]{1,0:T(8,128)(2,1)S(1)}, ...), branch_computations={%region_18.18_spmd, %region_19.22_spmd} | conditional | flops 1516831488 | bytes 79266456 | solution.py:177
  342.4 2.0 bitcast_dynamic-update-slice_fusion.11
  344.4 1.9 bitcast_dynamic-update-slice_fusion.10
  346.3 1.9 bitcast_dynamic-update-slice_fusion.9
  348.2 1.9 bitcast_dynamic-update-slice_fusion.8
  350.1 1.9 bitcast_dynamic-update-slice_fusion.7
  352.1 13.9 %add.389 = f32[5,768,768]{2,1,0:T(8,128)} add(f32[5,768,768]{2,1,0:T(8,128)} %get-tuple-element.1315, f32[5,768,768]{2,1,0:T(8,128)} %bitcast_dynamic-update-slice_fusion.7) | non-fusion elementwise | flops 2949120 | bytes 35389440 | tf_op jit(solution)/shard_map/while/body/eval_jaxpr/cond/branch_1_fun/add | solution.py:172
  368.3 2.1 fusion.108
  371.9 2.2 collective-permute-done.11
  374.3 4.6 collective-permute-start.10
  380.2 4.2 collective-permute-done.9
  384.4 28.2 %conditional.11 = (f32[5,768,768]{2,1,0:T(8,128)}, f32[768]{0:T(1024)S(1)}, bf16[128,768]{1,0:T(8,128)(2,1)S(1)}) conditional(s32[]{:T(128)} %convert_element_type.240, (f32[5,768,768]{2,1,0:T(8,128)}, f32[768]{0:T(1024)S(1)}) %tuple.226, (bf16[2,132,768]{2,1,0:T(8,128)(2,1)S(1)}, s32[]{:T(128)}, bf16[128,768]{1,0:T(8,128)(2,1)S(1)}, ...), branch_computations={%region_18.18_spmd, %region_19.22_spmd} | conditional | flops 1516831488 | bytes 79266456 | solution.py:177
  384.4 2.0 bitcast_dynamic-update-slice_fusion.11
  386.4 1.9 bitcast_dynamic-update-slice_fusion.10
  388.3 1.9 bitcast_dynamic-update-slice_fusion.9
  390.2 1.9 bitcast_dynamic-update-slice_fusion.8
  392.1 1.9 bitcast_dynamic-update-slice_fusion.7
  394.1 13.9 %add.389 = f32[5,768,768]{2,1,0:T(8,128)} add(f32[5,768,768]{2,1,0:T(8,128)} %get-tuple-element.1315, f32[5,768,768]{2,1,0:T(8,128)} %bitcast_dynamic-update-slice_fusion.7) | non-fusion elementwise | flops 2949120 | bytes 35389440 | tf_op jit(solution)/shard_map/while/body/eval_jaxpr/cond/branch_1_fun/add | solution.py:172
  410.3 2.1 fusion.108
  413.9 2.0 collective-permute-done.11
  415.9 7.4 %convert_element_type.184 = bf16[5,768,768]{2,1,0:T(8,128)(2,1)} convert(f32[5,768,768]{2,1,0:T(8,128)} %get-tuple-element.1365) | non-fusion elementwise | flops 2949120 | bytes 17694720 | tf_op jit(solution)/shard_map/convert_element_type | solution.py:202
  425.2 21.3 %all-reduce = bf16[768]{0:T(1024)(128)(2,1)S(1)} all-reduce(bf16[768]{0:T(1024)(128)(2,1)S(1)} %convert_element_type.185), channel_id=3, replica_groups=mesh['section'=4,'seq'=8] {'seq'}, use_global_device_ids=true, to_apply=%region_25.26.clone | all-reduce | flops 768 | bytes 3072
  447.1 89.2 %reduce-scatter.2.cloned.1.call-done = bf16[5,96,768]{2,1,0:T(8,128)(2,1)} async-done(((bf16[5,768,768]{2,1,0:T(8,128)(2,1)}), bf16[5,96,768]{2,1,0:T(8,128)(2,1)}) %reduce-scatter.2.cloned.1.call-update) | async-done | bytes 737296 | tf_op jit(solution)/shard_map/reduce_scatter | solution.py:201
  (200 shorter events, 71.6 us)
Async XLA Ops:
  7.2 529.1 %reduce-scatter.2.cloned.1.call-start = ((), (), s32[]{:S(2)}) async-start(), calls=%async_computation.5 | async-start | bytes 6635520 | tf_op jit(solution)/shard_map/reduce_scatter | solution.py:201
  8.0 7.7 %collective-permute-start.13 = (s32[2,7]{1,0:T(2,128)S(1)}, s32[2,7]{1,0:T(2,128)S(1)}, u32[]{:S(2)}, u32[]{:S(2)}) collective-permute-start(s32[2,7]{1,0:T(2,128)S(1)} %get-tuple-element.1503), channel_id=1, source_target_pairs={{1,0},{2,1},{3,2},{4,3},{5,4},{6,5},{7,6},{9,8},{10,9},{11,10},{12... | collective-permute-start | bytes 176 | tf_op jit(solution)/shard_map/ppermute | solution.py:19
  9.3 6.8 %collective-permute-start.12 = (s32[2,7]{1,0:T(2,128)S(1)}, s32[2,7]{1,0:T(2,128)S(1)}, u32[]{:S(2)}, u32[]{:S(2)}) collective-permute-start(s32[2,7]{1,0:T(2,128)S(1)} %get-tuple-element.1504), channel_id=1, source_target_pairs={{0,1},{1,2},{2,3},{3,4},{4,5},{5,6},{6,7},{8,9},{9,10},{10,11},{11... | collective-permute-start | bytes 176 | tf_op jit(solution)/shard_map/ppermute | solution.py:18
  18.2 6.8 %collective-permute-start = (bf16[2,768]{1,0:T(2,128)(2,1)S(1)}, bf16[2,768]{1,0:T(2,128)(2,1)S(1)}, u32[]{:S(2)}, u32[]{:S(2)}) collective-permute-start(bf16[2,768]{1,0:T(2,128)(2,1)S(1)} %get-tuple-element.1816), channel_id=1, source_target_pairs={{1,0},{2,1},{3,2},{4,3},{5,4},{6,5},{7,6},{9,8},{10,9},{11,10},{12... | collective-permute-start | bytes 9224 | tf_op jit(solution)/shard_map/while/body/eval_jaxpr/ppermute | solution.py:19
  19.5 6.8 %collective-permute-start.1 = (bf16[2,768]{1,0:T(2,128)(2,1)S(1)}, bf16[2,768]{1,0:T(2,128)(2,1)S(1)}, u32[]{:S(2)}, u32[]{:S(2)}) collective-permute-start(bf16[2,768]{1,0:T(2,128)(2,1)S(1)} %get-tuple-element.1817), channel_id=1, source_target_pairs={{0,1},{1,2},{2,3},{3,4},{4,5},{5,6},{6,7},{8,9},{9,10},{10,11},{11... | collective-permute-start | bytes 9224 | tf_op jit(solution)/shard_map/while/body/eval_jaxpr/ppermute | solution.py:18
  42.7 8.7 %all-to-all-start.1 = ((bf16[4,32,768]{2,1,0:T(8,128)(2,1)}), bf16[4,32,768]{2,1,0:T(8,128)(2,1)S(1)}, u32[]{:S(2)}, u32[]{:S(2)}) async-start(bf16[4,32,768]{2,1,0:T(8,128)(2,1)} %all_to_all.57), calls=%async_computation.1 | async-start | bytes 393216 | tf_op jit(solution)/shard_map/while/body/eval_jaxpr/all_to_all | solution.py:39
  46.4 5.1 collective-permute-start.2
  52.7 7.0 %collective-permute-start = (bf16[2,768]{1,0:T(2,128)(2,1)S(1)}, bf16[2,768]{1,0:T(2,128)(2,1)S(1)}, u32[]{:S(2)}, u32[]{:S(2)}) collective-permute-start(bf16[2,768]{1,0:T(2,128)(2,1)S(1)} %get-tuple-element.1816), channel_id=1, source_target_pairs={{1,0},{2,1},{3,2},{4,3},{5,4},{6,5},{7,6},{9,8},{10,9},{11,10},{12... | collective-permute-start | bytes 9224 | tf_op jit(solution)/shard_map/while/body/eval_jaxpr/ppermute | solution.py:19
  54.0 7.0 %collective-permute-start.1 = (bf16[2,768]{1,0:T(2,128)(2,1)S(1)}, bf16[2,768]{1,0:T(2,128)(2,1)S(1)}, u32[]{:S(2)}, u32[]{:S(2)}) collective-permute-start(bf16[2,768]{1,0:T(2,128)(2,1)S(1)} %get-tuple-element.1817), channel_id=1, source_target_pairs={{0,1},{1,2},{2,3},{3,4},{4,5},{5,6},{6,7},{8,9},{9,10},{10,11},{11... | collective-permute-start | bytes 9224 | tf_op jit(solution)/shard_map/while/body/eval_jaxpr/ppermute | solution.py:18
  77.6 8.7 %all-to-all-start.1 = ((bf16[4,32,768]{2,1,0:T(8,128)(2,1)}), bf16[4,32,768]{2,1,0:T(8,128)(2,1)S(1)}, u32[]{:S(2)}, u32[]{:S(2)}) async-start(bf16[4,32,768]{2,1,0:T(8,128)(2,1)} %all_to_all.57), calls=%async_computation.1 | async-start | bytes 393216 | tf_op jit(solution)/shard_map/while/body/eval_jaxpr/all_to_all | solution.py:39
  81.2 5.1 collective-permute-start.2
  87.6 7.0 %collective-permute-start = (bf16[2,768]{1,0:T(2,128)(2,1)S(1)}, bf16[2,768]{1,0:T(2,128)(2,1)S(1)}, u32[]{:S(2)}, u32[]{:S(2)}) collective-permute-start(bf16[2,768]{1,0:T(2,128)(2,1)S(1)} %get-tuple-element.1816), channel_id=1, source_target_pairs={{1,0},{2,1},{3,2},{4,3},{5,4},{6,5},{7,6},{9,8},{10,9},{11,10},{12... | collective-permute-start | bytes 9224 | tf_op jit(solution)/shard_map/while/body/eval_jaxpr/ppermute | solution.py:19
  88.9 7.0 %collective-permute-start.1 = (bf16[2,768]{1,0:T(2,128)(2,1)S(1)}, bf16[2,768]{1,0:T(2,128)(2,1)S(1)}, u32[]{:S(2)}, u32[]{:S(2)}) collective-permute-start(bf16[2,768]{1,0:T(2,128)(2,1)S(1)} %get-tuple-element.1817), channel_id=1, source_target_pairs={{0,1},{1,2},{2,3},{3,4},{4,5},{5,6},{6,7},{8,9},{9,10},{10,11},{11... | collective-permute-start | bytes 9224 | tf_op jit(solution)/shard_map/while/body/eval_jaxpr/ppermute | solution.py:18
  114.9 8.7 %all-to-all-start.1 = ((bf16[4,32,768]{2,1,0:T(8,128)(2,1)}), bf16[4,32,768]{2,1,0:T(8,128)(2,1)S(1)}, u32[]{:S(2)}, u32[]{:S(2)}) async-start(bf16[4,32,768]{2,1,0:T(8,128)(2,1)} %all_to_all.57), calls=%async_computation.1 | async-start | bytes 393216 | tf_op jit(solution)/shard_map/while/body/eval_jaxpr/all_to_all | solution.py:39
  118.5 5.1 collective-permute-start.2
  124.9 7.0 %collective-permute-start.3 = (bf16[2,768]{1,0:T(2,128)(2,1)S(1)}, bf16[2,768]{1,0:T(2,128)(2,1)S(1)}, u32[]{:S(2)}, u32[]{:S(2)}) collective-permute-start(bf16[2,768]{1,0:T(2,128)(2,1)S(1)} %get-tuple-element.1832), channel_id=1, source_target_pairs={{1,0},{2,1},{3,2},{4,3},{5,4},{6,5},{7,6},{9,8},{10,9},{11,10},{12... | collective-permute-start | bytes 9224 | tf_op jit(solution)/shard_map/while/body/eval_jaxpr/ppermute | solution.py:19
  126.2 7.0 %collective-permute-start.4 = (bf16[2,768]{1,0:T(2,128)(2,1)S(1)}, bf16[2,768]{1,0:T(2,128)(2,1)S(1)}, u32[]{:S(2)}, u32[]{:S(2)}) collective-permute-start(bf16[2,768]{1,0:T(2,128)(2,1)S(1)} %get-tuple-element.1833), channel_id=1, source_target_pairs={{0,1},{1,2},{2,3},{3,4},{4,5},{5,6},{6,7},{8,9},{9,10},{10,11},{11... | collective-permute-start | bytes 9224 | tf_op jit(solution)/shard_map/while/body/eval_jaxpr/ppermute | solution.py:18
  133.4 3.6 collective-permute-start.5
  138.1 7.0 %collective-permute-start.3 = (bf16[2,768]{1,0:T(2,128)(2,1)S(1)}, bf16[2,768]{1,0:T(2,128)(2,1)S(1)}, u32[]{:S(2)}, u32[]{:S(2)}) collective-permute-start(bf16[2,768]{1,0:T(2,128)(2,1)S(1)} %get-tuple-element.1832), channel_id=1, source_target_pairs={{1,0},{2,1},{3,2},{4,3},{5,4},{6,5},{7,6},{9,8},{10,9},{11,10},{12... | collective-permute-start | bytes 9224 | tf_op jit(solution)/shard_map/while/body/eval_jaxpr/ppermute | solution.py:19
  139.4 7.0 %collective-permute-start.4 = (bf16[2,768]{1,0:T(2,128)(2,1)S(1)}, bf16[2,768]{1,0:T(2,128)(2,1)S(1)}, u32[]{:S(2)}, u32[]{:S(2)}) collective-permute-start(bf16[2,768]{1,0:T(2,128)(2,1)S(1)} %get-tuple-element.1833), channel_id=1, source_target_pairs={{0,1},{1,2},{2,3},{3,4},{4,5},{5,6},{6,7},{8,9},{9,10},{10,11},{11... | collective-permute-start | bytes 9224 | tf_op jit(solution)/shard_map/while/body/eval_jaxpr/ppermute | solution.py:18
  146.6 15.0 %collective-permute-start.5 = (bf16[128,768]{1,0:T(8,128)(2,1)S(1)}, bf16[128,768]{1,0:T(8,128)(2,1)S(1)}, u32[]{:S(2)}, u32[]{:S(2)}) collective-permute-start(bf16[128,768]{1,0:T(8,128)(2,1)S(1)} %get-tuple-element.2089), channel_id=1, source_target_pairs={{0,8},{8,16},{16,24},{1,9},{9,17},{17,25},{2,10},{10,18},{18,26},{... | collective-permute-start | bytes 589832 | tf_op jit(solution)/shard_map/while/body/eval_jaxpr/ppermute | solution.py:27
  161.6 5.5 %copy-start = (bf16[2,128,768]{2,1,0:T(8,128)(2,1)S(1)}, bf16[2,128,768]{2,1,0:T(8,128)(2,1)}, u32[]{:S(2)}) copy-start(bf16[2,128,768]{2,1,0:T(8,128)(2,1)} %param.25) | copy-start | bytes 1179652
  161.6 5.5 %copy-start.1 = (f32[1,768]{1,0:T(1,128)S(1)}, f32[1,768]{1,0:T(1,128)}, u32[]{:S(2)}) copy-start(f32[1,768]{1,0:T(1,128)} %get-tuple-element.2111) | copy-start | bytes 9220
  167.2 7.0 %collective-permute-start.6 = (bf16[2,768]{1,0:T(2,128)(2,1)S(1)}, bf16[2,768]{1,0:T(2,128)(2,1)S(1)}, u32[]{:S(2)}, u32[]{:S(2)}) collective-permute-start(bf16[2,768]{1,0:T(2,128)(2,1)S(1)} %get-tuple-element.1849), channel_id=1, source_target_pairs={{1,0},{2,1},{3,2},{4,3},{5,4},{6,5},{7,6},{9,8},{10,9},{11,10},{12... | collective-permute-start | bytes 9224 | tf_op jit(solution)/shard_map/while/body/eval_jaxpr/ppermute | solution.py:19
  168.5 7.0 %collective-permute-start.7 = (bf16[2,768]{1,0:T(2,128)(2,1)S(1)}, bf16[2,768]{1,0:T(2,128)(2,1)S(1)}, u32[]{:S(2)}, u32[]{:S(2)}) collective-permute-start(bf16[2,768]{1,0:T(2,128)(2,1)S(1)} %get-tuple-element.1850), channel_id=1, source_target_pairs={{0,1},{1,2},{2,3},{3,4},{4,5},{5,6},{6,7},{8,9},{9,10},{10,11},{11... | collective-permute-start | bytes 9224 | tf_op jit(solution)/shard_map/while/body/eval_jaxpr/ppermute | solution.py:18
  213.2 8.7 %all-to-all-start.3 = ((bf16[4,32,768]{2,1,0:T(8,128)(2,1)}), bf16[4,32,768]{2,1,0:T(8,128)(2,1)S(1)}, u32[]{:S(2)}, u32[]{:S(2)}) async-start(bf16[4,32,768]{2,1,0:T(8,128)(2,1)} %all_to_all.60), calls=%async_computation.3 | async-start | bytes 393216 | tf_op jit(solution)/shard_map/while/body/eval_jaxpr/all_to_all | solution.py:39
  216.6 5.3 collective-permute-start.8
  222.1 7.0 %collective-permute-start.6 = (bf16[2,768]{1,0:T(2,128)(2,1)S(1)}, bf16[2,768]{1,0:T(2,128)(2,1)S(1)}, u32[]{:S(2)}, u32[]{:S(2)}) collective-permute-start(bf16[2,768]{1,0:T(2,128)(2,1)S(1)} %get-tuple-element.1849), channel_id=1, source_target_pairs={{1,0},{2,1},{3,2},{4,3},{5,4},{6,5},{7,6},{9,8},{10,9},{11,10},{12... | collective-permute-start | bytes 9224 | tf_op jit(solution)/shard_map/while/body/eval_jaxpr/ppermute | solution.py:19
  223.4 7.0 %collective-permute-start.7 = (bf16[2,768]{1,0:T(2,128)(2,1)S(1)}, bf16[2,768]{1,0:T(2,128)(2,1)S(1)}, u32[]{:S(2)}, u32[]{:S(2)}) collective-permute-start(bf16[2,768]{1,0:T(2,128)(2,1)S(1)} %get-tuple-element.1850), channel_id=1, source_target_pairs={{0,1},{1,2},{2,3},{3,4},{4,5},{5,6},{6,7},{8,9},{9,10},{10,11},{11... | collective-permute-start | bytes 9224 | tf_op jit(solution)/shard_map/while/body/eval_jaxpr/ppermute | solution.py:18
  267.5 8.7 %all-to-all-start.3 = ((bf16[4,32,768]{2,1,0:T(8,128)(2,1)}), bf16[4,32,768]{2,1,0:T(8,128)(2,1)S(1)}, u32[]{:S(2)}, u32[]{:S(2)}) async-start(bf16[4,32,768]{2,1,0:T(8,128)(2,1)} %all_to_all.60), calls=%async_computation.3 | async-start | bytes 393216 | tf_op jit(solution)/shard_map/while/body/eval_jaxpr/all_to_all | solution.py:39
  270.9 5.3 collective-permute-start.8
  276.4 6.8 %collective-permute-start.6 = (bf16[2,768]{1,0:T(2,128)(2,1)S(1)}, bf16[2,768]{1,0:T(2,128)(2,1)S(1)}, u32[]{:S(2)}, u32[]{:S(2)}) collective-permute-start(bf16[2,768]{1,0:T(2,128)(2,1)S(1)} %get-tuple-element.1849), channel_id=1, source_target_pairs={{1,0},{2,1},{3,2},{4,3},{5,4},{6,5},{7,6},{9,8},{10,9},{11,10},{12... | collective-permute-start | bytes 9224 | tf_op jit(solution)/shard_map/while/body/eval_jaxpr/ppermute | solution.py:19
  277.7 6.8 %collective-permute-start.7 = (bf16[2,768]{1,0:T(2,128)(2,1)S(1)}, bf16[2,768]{1,0:T(2,128)(2,1)S(1)}, u32[]{:S(2)}, u32[]{:S(2)}) collective-permute-start(bf16[2,768]{1,0:T(2,128)(2,1)S(1)} %get-tuple-element.1850), channel_id=1, source_target_pairs={{0,1},{1,2},{2,3},{3,4},{4,5},{5,6},{6,7},{8,9},{9,10},{10,11},{11... | collective-permute-start | bytes 9224 | tf_op jit(solution)/shard_map/while/body/eval_jaxpr/ppermute | solution.py:18
  321.5 8.7 %all-to-all-start.3 = ((bf16[4,32,768]{2,1,0:T(8,128)(2,1)}), bf16[4,32,768]{2,1,0:T(8,128)(2,1)S(1)}, u32[]{:S(2)}, u32[]{:S(2)}) async-start(bf16[4,32,768]{2,1,0:T(8,128)(2,1)} %all_to_all.60), calls=%async_computation.3 | async-start | bytes 393216 | tf_op jit(solution)/shard_map/while/body/eval_jaxpr/all_to_all | solution.py:39
  324.9 5.3 collective-permute-start.8
  330.6 6.4 %collective-permute-start.10 = (bf16[2,768]{1,0:T(2,128)(2,1)S(1)}, bf16[2,768]{1,0:T(2,128)(2,1)S(1)}, u32[]{:S(2)}, u32[]{:S(2)}) collective-permute-start(bf16[2,768]{1,0:T(2,128)(2,1)S(1)} %get-tuple-element.1868), channel_id=1, source_target_pairs={{0,1},{1,2},{2,3},{3,4},{4,5},{5,6},{6,7},{8,9},{9,10},{10,11},{11... | collective-permute-start | bytes 9224 | tf_op jit(solution)/shard_map/while/body/eval_jaxpr/ppermute | solution.py:18
  335.7 6.7 %collective-permute-start.9 = (bf16[2,768]{1,0:T(2,128)(2,1)S(1)}, bf16[2,768]{1,0:T(2,128)(2,1)S(1)}, u32[]{:S(2)}, u32[]{:S(2)}) collective-permute-start(bf16[2,768]{1,0:T(2,128)(2,1)S(1)} %get-tuple-element.1867), channel_id=1, source_target_pairs={{1,0},{2,1},{3,2},{4,3},{5,4},{6,5},{7,6},{9,8},{10,9},{11,10},{12... | collective-permute-start | bytes 9224 | tf_op jit(solution)/shard_map/while/body/eval_jaxpr/ppermute | solution.py:19
  350.1 15.8 %slice-start.2 = ((s8[5898240]{0:T(1024)(128)(4,1)}), s8[4194304]{0:T(1024)(128)(4,1)S(1)}, s32[]{:S(2)}) async-start(s8[5898240]{0:T(1024)(128)(4,1)} %bitcast.277), calls=%async_computation.8 | async-start | bytes 8388608 | tf_op jit(solution)/shard_map/while/body/eval_jaxpr/cond
  352.1 13.9 %slice-start.3 = ((s8[5898240]{0:T(1024)(128)(4,1)}), s8[1703936]{0:T(1024)(128)(4,1)S(1)}, s32[]{:S(2)}) async-start(s8[5898240]{0:T(1024)(128)(4,1)} %bitcast.277), calls=%async_computation.9 | async-start | bytes 3407872 | tf_op jit(solution)/shard_map/while/body/eval_jaxpr/cond
  370.6 3.5 collective-permute-start.11
  374.3 5.9 %collective-permute-start.10 = (bf16[2,768]{1,0:T(2,128)(2,1)S(1)}, bf16[2,768]{1,0:T(2,128)(2,1)S(1)}, u32[]{:S(2)}, u32[]{:S(2)}) collective-permute-start(bf16[2,768]{1,0:T(2,128)(2,1)S(1)} %get-tuple-element.1868), channel_id=1, source_target_pairs={{0,1},{1,2},{2,3},{3,4},{4,5},{5,6},{6,7},{8,9},{9,10},{10,11},{11... | collective-permute-start | bytes 9224 | tf_op jit(solution)/shard_map/while/body/eval_jaxpr/ppermute | solution.py:18
  378.9 5.5 %collective-permute-start.9 = (bf16[2,768]{1,0:T(2,128)(2,1)S(1)}, bf16[2,768]{1,0:T(2,128)(2,1)S(1)}, u32[]{:S(2)}, u32[]{:S(2)}) collective-permute-start(bf16[2,768]{1,0:T(2,128)(2,1)S(1)} %get-tuple-element.1867), channel_id=1, source_target_pairs={{1,0},{2,1},{3,2},{4,3},{5,4},{6,5},{7,6},{9,8},{10,9},{11,10},{12... | collective-permute-start | bytes 9224 | tf_op jit(solution)/shard_map/while/body/eval_jaxpr/ppermute | solution.py:19
  392.1 15.8 %slice-start.2 = ((s8[5898240]{0:T(1024)(128)(4,1)}), s8[4194304]{0:T(1024)(128)(4,1)S(1)}, s32[]{:S(2)}) async-start(s8[5898240]{0:T(1024)(128)(4,1)} %bitcast.277), calls=%async_computation.8 | async-start | bytes 8388608 | tf_op jit(solution)/shard_map/while/body/eval_jaxpr/cond
  394.1 13.9 %slice-start.3 = ((s8[5898240]{0:T(1024)(128)(4,1)}), s8[1703936]{0:T(1024)(128)(4,1)S(1)}, s32[]{:S(2)}) async-start(s8[5898240]{0:T(1024)(128)(4,1)} %bitcast.277), calls=%async_computation.9 | async-start | bytes 3407872 | tf_op jit(solution)/shard_map/while/body/eval_jaxpr/cond
  412.6 3.3 collective-permute-start.11
  423.3 0.7 copy-start.2
Sparse Core Ops, SparseCore 0:
  423.5 112.7 reduce-scatter.1
where the time goes:
time: 545 us; the launch traced here: 543 us
  blocking collectives  164 us (30%)
  waiting for transfers between devices  135 us (25%)
  starting transfers between devices  125 us (23%)
  other arithmetic  46.1 us (8%)
  matrix products  44.1 us (8%)
  between operations  14.9 us (3%)
  local copies, waits for them, and re-layouts  12.5 us (2%)
    all_to_all x6, blocking collectives, mirror(): lax.all_to_all(payload, 'section', split_axis=0, concat_axis=0, tiled=True)  143 us
    reduce_scatter x1, waiting for transfers between devices, shards(): lax.psum_scatter(kernel_sum.astype(jnp.bfloat16), 'seq', scatter_dimensio...  89.2 us
    ppermute x11, starting transfers between devices, padded_2(): before = lax.ppermute(last, axis, up)  60.3 us
    ppermute x10, starting transfers between devices, passed_along(): return lax.ppermute(block, axis, route)  30.1 us
    add x4, other arithmetic, backward_block(): return (kernel_sum + kernel_terms, gain_sum + grad_gain, grad_in)  27.8 us
    unnamed x1, blocking collectives  21.3 us
    all_to_all x6, starting transfers between devices, mirror(): lax.all_to_all(flipped, 'section', split_axis=0, concat_axis=0, tiled=True)  20.2 us
    all_to_all x6, waiting for transfers between devices, mirror(): lax.all_to_all(flipped, 'section', split_axis=0, concat_axis=0, tiled=True)  19.6 us
  transfers between devices with their start and end apart: 39, of which 22 were waited for; matrix products, arithmetic and copies ran while one was open for 1% of the time, Pallas kernels for 0%

commit v1 on v0

v1 whole, which is shorter than its diff:
```python
import functools

import jax
import jax.numpy as jnp
from jax import lax
from jax.experimental import pallas as pl
from jax.experimental.pallas import tpu as pltpu
from jax.sharding import PartitionSpec as P

KERNEL = 5
STEM_K = 15
BASES = 4
LANES = 128
EDGE = 8
F32, BF16 = jnp.float32, jnp.bfloat16
GELU_A, GELU_B = 0.7978845608028654, 0.044715


def remote(src, dst, send_sem, recv_sem, **where):
    return pltpu.make_async_remote_copy(
        src_ref=src,
        dst_ref=dst,
        send_sem=send_sem,
        recv_sem=recv_sem,
        device_id=where,
        device_id_type=pl.DeviceIdType.MESH,
    )


def level_kernel(
    sections, n_seq, n_lo, micro, rows, chans, halo,
    e_ref, stem_ref, w_ref, gain_ref, cot_ref,
    out_ref, gout_ref,
    ebuf, bsum, actf, x5, gradf, gact, inflow, skip, fout, gin, gskip, gsend, coth,
    aslab, acol, acolf, a5t, gall, acc, gain_acc, gslab, grecv,
    e_send, e_recv, c_send, c_recv, f_send, f_recv, b_send, b_recv,
    a_send, a_recv, n_send, n_recv, ag_send, ag_recv,
):
    sec, q = lax.axis_index("section"), lax.axis_index("seq")
    n_hi = n_seq // n_lo
    hi, lo = q // n_lo, q % n_lo
    half = sections // 2
    ext = rows + 2 * halo
    e_halo = halo + 16
    part = chans // n_seq
    reach = (KERNEL - 1) // 2
    last = sections - 1
    mirror_sec = last - sec
    step = 32
    tokens = rows * n_seq

    barrier = pltpu.get_barrier_semaphore()
    for d in range(1, n_seq):
        pl.semaphore_signal(
            barrier, inc=1, device_id={"seq": (q + d) % n_seq}, device_id_type=pl.DeviceIdType.MESH
        )
    for d in range(1, sections):
        pl.semaphore_signal(
            barrier, inc=1, device_id={"section": (sec + d) % sections},
            device_id_type=pl.DeviceIdType.MESH,
        )
    pl.semaphore_wait(barrier, n_seq + sections - 2)

    def e_copy(side):
        if side == 0:
            src, dst, to = e_ref.at[:, rows - e_halo : rows], ebuf.at[:, 0:e_halo], q + 1
        else:
            src, dst, to = e_ref.at[:, 0:e_halo], ebuf.at[:, e_halo + rows :], q - 1
        return remote(src, dst, e_send.at[side], e_recv.at[side], seq=to)

    def c_copy(side):
        if side == 0:
            src, dst, to = cot_ref.at[:, rows - halo : rows], coth.at[0], q + 1
        else:
            src, dst, to = cot_ref.at[:, 0:halo], coth.at[1], q - 1
        return remote(src, dst, c_send.at[side], c_recv.at[side], seq=to)

    def gather_copy(block, m, way):
        to = [q + n_lo, q - n_lo, q + 1, q - 1][way]
        return remote(
            gall.at[block, m], gall.at[block, m], ag_send.at[block, m, way],
            ag_recv.at[block, m], seq=to,
        )

    up, down, right, left = hi < n_hi - 1, hi > 0, lo < n_lo - 1, lo > 0

    def each_way(ways, block, m, act):
        for way in ways:
            @pl.when([up, down, right, left][way])
            def _():
                act(gather_copy(block, m, way))

    def start(copy):
        copy.start()

    def wait_send(copy):
        copy.wait_send()

    for ref in (actf, gradf):
        ref[:, 0:EDGE] = jnp.zeros((micro, EDGE, chans), F32)
        ref[:, EDGE + ext :] = jnp.zeros((micro, EDGE, chans), F32)
    acolf[:, 0:EDGE] = jnp.zeros((micro, EDGE, LANES), F32)
    acolf[:, EDGE + tokens :] = jnp.zeros((micro, EDGE, LANES), F32)
    gain_acc[...] = jnp.zeros_like(gain_acc)

    @pl.when(sec == 0)
    def _():
        @pl.when(q < n_seq - 1)
        def _():
            e_copy(0).start()

        @pl.when(q > 0)
        def _():
            e_copy(1).start()

        ebuf[:, e_halo : e_halo + rows] = e_ref[...]

        @pl.when(q == 0)
        def _():
            ebuf[:, 0:e_halo] = jnp.zeros((micro, e_halo, LANES), F32)

        @pl.when(q == n_seq - 1)
        def _():
            ebuf[:, e_halo + rows :] = jnp.zeros((micro, e_halo, LANES), F32)

        @pl.when(q > 0)
        def _():
            e_copy(0).wait_recv()

        @pl.when(q < n_seq - 1)
        def _():
            e_copy(1).wait_recv()

    def row_mask(first, count):
        place = lax.broadcasted_iota(jnp.int32, (count, 1), 0) + (first + q * rows - halo)
        return (place >= 0) & (place < tokens)

    def shifted(ref, m, flip):
        for k in range(KERNEL):
            off = EDGE + (reach - k if flip else k - reach)
            x5[:, k * chans : (k + 1) * chans] = ref[m, off : off + ext].astype(BF16)

    def conv_back(m):
        shifted(gradf, m, True)

        def tile(n, carry):
            at = pl.ds(pl.multiple_of(n * 256, 256), 256)
            total = jnp.zeros((ext, 256), F32)
            for k in range(KERNEL):
                total = total + lax.dot_general(
                    x5[:, k * chans : (k + 1) * chans],
                    w_ref[pl.ds(pl.multiple_of(k * chans + n * 256, 256), 256), :],
                    (((1,), (1,)), ((), ())),
                    preferred_element_type=F32,
                )
            gact[m, :, at] = total
            return carry

        lax.fori_loop(0, chans // 256, tile, 0)

    @pl.when(sec == last)
    def _():
        @pl.when(q < n_seq - 1)
        def _():
            c_copy(0).start()

        @pl.when(q > 0)
        def _():
            c_copy(1).start()

        gall[q] = cot_ref[...]
        for m in range(micro):
            each_way(range(4), q, m, start)
        gradf[:, EDGE + halo : EDGE + halo + rows] = cot_ref[...].astype(F32)

        @pl.when(q == 0)
        def _():
            gradf[:, EDGE : EDGE + halo] = jnp.zeros((micro, halo, chans), F32)

        @pl.when(q == n_seq - 1)
        def _():
            gradf[:, EDGE + halo + rows : EDGE + ext] = jnp.zeros((micro, halo, chans), F32)

        @pl.when(q > 0)
        def _():
            c_copy(0).wait_recv()
            gradf[:, EDGE : EDGE + halo] = coth[0].astype(F32)

        @pl.when(q < n_seq - 1)
        def _():
            c_copy(1).wait_recv()
            gradf[:, EDGE + halo + rows : EDGE + ext] = coth[1].astype(F32)

        def each(m, carry):
            conv_back(m)
            return carry

        lax.fori_loop(0, micro, each, 0)

    def f_copy(m, kind):
        to = sec + 1 if kind == 0 else mirror_sec
        dst = inflow if kind == 0 else skip
        return remote(fout.at[m], dst.at[m], f_send.at[m, kind], f_recv.at[m, kind], section=to)

    def b_copy(m, kind):
        to = sec - 1 if kind == 0 else mirror_sec
        dst = gin if kind == 0 else gskip
        return remote(gsend.at[m], dst.at[m], b_send.at[m, kind], b_recv.at[m, kind], section=to)

    def by_rows(body):
        def one(i, carry):
            body(pl.multiple_of(i * step, step))
            return carry

        lax.fori_loop(0, ext // step, one, 0)

    def forward(m, carry):
        @pl.when(sec == 0)
        def _():
            tap = lax.broadcasted_iota(jnp.int32, (ext, LANES), 1) // BASES
            hot = jnp.zeros((ext, LANES), F32)
            for k in range(STEM_K):
                off = e_halo - halo + k - (STEM_K - 1) // 2
                hot = jnp.where(tap == k, ebuf[m, off : off + ext], hot)
            stem = jnp.dot(hot.astype(BF16), stem_ref[...], preferred_element_type=F32)
            bsum[m] = stem.astype(BF16).astype(F32)

        @pl.when(sec > 0)
        def _():
            f_copy(m, 0).wait_recv()

            @pl.when(sec < half)
            def _():
                bsum[m] = inflow[m].astype(F32)

            @pl.when(sec == half)
            def _():
                bsum[m] = inflow[m].astype(F32) * 2.0

            @pl.when(sec > half)
            def _():
                f_copy(m, 1).wait_recv()
                bsum[m] = inflow[m].astype(F32) + skip[m].astype(F32)

        def act_rows(r):
            b = bsum[m, pl.ds(r, step)]
            scale = lax.rsqrt(jnp.mean(b * b, axis=-1, keepdims=True) + 1e-06)
            x = b * scale * gain_ref[...]
            t = jnp.tanh(GELU_A * (x + GELU_B * (x * x * x)))
            y = (x * (0.5 * (1.0 + t))).astype(BF16).astype(F32)
            actf[m, pl.ds(pl.multiple_of(EDGE + r, 8), step)] = jnp.where(row_mask(r, step), y, 0.0)

        by_rows(act_rows)

        @pl.when(sec < last)
        def _():
            shifted(actf, m, False)

            def tile(n, c):
                at = pl.ds(pl.multiple_of(n * 256, 256), 256)
                total = bsum[m, :, at] + jnp.dot(
                    x5[...], w_ref[:, at], preferred_element_type=F32
                )
                fout[m, :, at] = total.astype(BF16)
                return c

            lax.fori_loop(0, chans // 256, tile, 0)
            f_copy(m, 0).start()

            @pl.when(sec < half - 1)
            def _():
                f_copy(m, 1).start()

        return carry

    lax.fori_loop(0, micro, forward, 0)

    def picker(j):
        c = lax.broadcasted_iota(jnp.int32, (chans, LANES), 0)
        lane = lax.broadcasted_iota(jnp.int32, (chans, LANES), 1)
        return jnp.where((c == j * part + lane) & (lane < part), 1.0, 0.0).astype(BF16)

    def a_copy(j):
        return remote(aslab.at[j], acol.at[q], a_send.at[j], a_recv.at[q], seq=j)

    def a_from(j):
        return remote(aslab.at[j], acol.at[j], a_send.at[j], a_recv.at[j], seq=j)

    def spread_rows():
        own = slice(EDGE + halo, EDGE + halo + rows)

        def slab(j, carry):
            pick = picker(j)
            for m in range(micro):
                aslab[j, m] = jnp.dot(
                    actf[m, own].astype(BF16), pick, preferred_element_type=F32
                ).astype(BF16)

            @pl.when(j != q)
            def _():
                a_copy(j).start()

            @pl.when(j == q)
            def _():
                acol[j] = aslab[j]

            return carry

        lax.fori_loop(0, n_seq, slab, 0)

        def take(j, carry):
            @pl.when(j != q)
            def _():
                a_from(j).wait_recv()

            at = pl.ds(pl.multiple_of(EDGE + j * rows, 8), rows)
            for m in range(micro):
                acolf[m, at] = acol[j, m].astype(F32)
            return carry

        lax.fori_loop(0, n_seq, take, 0)

        def turn(j, carry):
            for m in range(micro):
                window = acolf[m, pl.ds(pl.multiple_of(j * rows, rows), rows + 2 * EDGE)]
                for k in range(KERNEL):
                    off = EDGE + k - reach
                    a5t[j, k * LANES : (k + 1) * LANES, m * rows : (m + 1) * rows] = (
                        window[off : off + rows].T.astype(BF16)
                    )
            return carry

        lax.fori_loop(0, n_seq, turn, 0)

    @pl.when(sec < half)
    def _():
        spread_rows()

    def backward(m, carry):
        @pl.when(sec < last)
        def _():
            b_copy(m, 0).wait_recv()

            @pl.when(sec < half - 1)
            def _():
                b_copy(m, 1).wait_recv()
                gradf[m, EDGE : EDGE + ext] = (
                    (gin[m].astype(F32) + gskip[m].astype(F32)).astype(BF16).astype(F32)
                )

            @pl.when(sec == half - 1)
            def _():
                gradf[m, EDGE : EDGE + ext] = gin[m].astype(F32) * 2.0

            @pl.when(sec >= half)
            def _():
                gradf[m, EDGE : EDGE + ext] = gin[m].astype(F32)

            gall[q, m] = gradf[m, EDGE + halo : EDGE + halo + rows].astype(BF16)
            each_way(range(4), q, m, start)
            conv_back(m)

        def pull_rows(r):
            at = pl.ds(r, step)
            b, grad = bsum[m, at], gact[m, at]
            scale = lax.rsqrt(jnp.mean(b * b, axis=-1, keepdims=True) + 1e-06)
            unit = b * scale
            x = unit * gain_ref[...]
            t = jnp.tanh(GELU_A * (x + GELU_B * (x * x * x)))
            slope = 0.5 * (1.0 + t) + (0.5 * GELU_A) * x * (1.0 - t * t) * (
                1.0 + (3.0 * GELU_B) * (x * x)
            )
            d_pre = grad * slope
            d_unit = d_pre * gain_ref[...]
            place = lax.broadcasted_iota(jnp.int32, (step, 1), 0) + r
            mine = (place >= halo) & (place < halo + rows)
            terms = jnp.where(mine, d_pre * unit, 0.0)
            gain_acc[...] += jnp.sum(terms.reshape(step // 8, 8, chans), axis=0)
            pulled = scale * (d_unit - unit * jnp.mean(d_unit * unit, axis=-1, keepdims=True))
            whole = gradf[m, pl.ds(pl.multiple_of(EDGE + r, 8), step)] + pulled
            gsend[m, at] = jnp.where(row_mask(r, step), whole, 0.0).astype(BF16)

        by_rows(pull_rows)

        @pl.when(sec > 0)
        def _():
            b_copy(m, 0).start()

            @pl.when(sec > half)
            def _():
                b_copy(m, 1).start()

        return carry

    lax.fori_loop(0, micro, backward, 0)

    for d in range(1, n_hi):
        for m in range(micro):
            @pl.when(hi - d >= 0)
            def _():
                block = q - d * n_lo
                gather_copy(block, m, 0).wait_recv()
                each_way((0, 2, 3), block, m, start)

            @pl.when(hi + d < n_hi)
            def _():
                block = q + d * n_lo
                gather_copy(block, m, 1).wait_recv()
                each_way((1, 2, 3), block, m, start)

    @pl.when(sec >= half)
    def _():
        spread_rows()

    def n_copy(j):
        return remote(gslab.at[j], grecv.at[q], n_send.at[j], n_recv.at[q], seq=j)

    def n_from(j):
        return remote(gslab.at[j], grecv.at[j], n_send.at[j], n_recv.at[j], seq=j)

    gain_part = jnp.broadcast_to(jnp.sum(gain_acc[...], axis=0, keepdims=True), (16, chans))
    gain_part = gain_part.astype(BF16)

    def gain_slab(j, carry):
        gslab[j] = jnp.dot(gain_part, picker(j), preferred_element_type=F32)[0:8]

        @pl.when(j != q)
        def _():
            n_copy(j).start()

        @pl.when(j == q)
        def _():
            grecv[j] = gslab[j]

        return carry

    lax.fori_loop(0, n_seq, gain_slab, 0)

    for e in range(1, n_lo):
        for h in range(n_hi):
            for m in range(micro):
                @pl.when(lo - e >= 0)
                def _():
                    block = h * n_lo + lo - e
                    gather_copy(block, m, 2).wait_recv()
                    each_way((2,), block, m, start)

                @pl.when(lo + e < n_lo)
                def _():
                    block = h * n_lo + lo + e
                    gather_copy(block, m, 3).wait_recv()
                    each_way((3,), block, m, start)

    acc[...] = jnp.zeros_like(acc)

    def multiply(j, carry):
        def tile(n, c):
            at = pl.ds(pl.multiple_of(n * 256, 256), 256)
            acc[:, at] += jnp.dot(
                a5t[j], gall[j, :, :, at].reshape(micro * rows, 256), preferred_element_type=F32
            )
            return c

        return lax.fori_loop(0, chans // 256, tile, carry)

    lax.fori_loop(0, n_seq, multiply, 0)
    for k in range(KERNEL):
        out_ref[k] = acc[k * LANES : k * LANES + part].astype(BF16)

    def gain_take(j, total):
        @pl.when(j != q)
        def _():
            n_from(j).wait_recv()

        return total + grecv[j]

    gain_total = lax.fori_loop(0, n_seq, gain_take, jnp.zeros((8, LANES), F32))
    gout_ref[...] = gain_total[0:1, 0:part]

    @pl.when(sec == 0)
    def _():
        @pl.when(q < n_seq - 1)
        def _():
            e_copy(0).wait_send()

        @pl.when(q > 0)
        def _():
            e_copy(1).wait_send()

    @pl.when(sec == last)
    def _():
        @pl.when(q < n_seq - 1)
        def _():
            c_copy(0).wait_send()

        @pl.when(q > 0)
        def _():
            c_copy(1).wait_send()

    for m in range(micro):
        @pl.when(sec < last)
        def _():
            f_copy(m, 0).wait_send()

        @pl.when(sec < half - 1)
        def _():
            f_copy(m, 1).wait_send()

        @pl.when(sec > 0)
        def _():
            b_copy(m, 0).wait_send()

        @pl.when(sec > half)
        def _():
            b_copy(m, 1).wait_send()

        each_way(range(4), q, m, wait_send)
        for d in range(1, n_hi):
            @pl.when(hi - d >= 0)
            def _():
                each_way((0, 2, 3), q - d * n_lo, m, wait_send)

            @pl.when(hi + d < n_hi)
            def _():
                each_way((1, 2, 3), q + d * n_lo, m, wait_send)

        for e in range(1, n_lo):
            for h in range(n_hi):
                @pl.when(lo - e >= 0)
                def _():
                    each_way((2,), h * n_lo + lo - e, m, wait_send)

                @pl.when(lo + e < n_lo)
                def _():
                    each_way((3,), h * n_lo + lo + e, m, wait_send)

    def sent(j, carry):
        @pl.when(j != q)
        def _():
            a_copy(j).wait_send()
            n_copy(j).wait_send()

        return carry

    lax.fori_loop(0, n_seq, sent, 0)


def shards(sections, n_seq, base_ids, stem_weight, conv_weight, block_gain, cotangent):
    micro, rows, chans = cotangent.shape
    n_lo = max(1, n_seq // 4)
    halo = -(-4 * (sections - 1) // 16) * 16
    ext = rows + 2 * halo
    e_halo = halo + 16
    part = chans // n_seq
    taps = STEM_K * BASES
    lane = jnp.arange(LANES, dtype=jnp.int32)
    wanted = jnp.where(lane < taps, lane % BASES, -1)
    spread = (base_ids[:, :, None] == wanted).astype(F32)
    stem = jnp.pad(stem_weight.reshape(taps, chans), ((0, LANES - taps), (0, 0)))
    vmem, dma = pltpu.VMEM, pltpu.SemaphoreType.DMA
    flow = vmem((micro, ext, chans), BF16)
    scratch = [
        vmem((micro, rows + 2 * e_halo, LANES), F32),
        vmem((micro, ext, chans), F32),
        vmem((micro, ext + 2 * EDGE, chans), F32),
        vmem((ext, KERNEL * chans), BF16),
        vmem((micro, ext + 2 * EDGE, chans), F32),
        vmem((micro, ext, chans), F32),
        flow, flow, flow, flow, flow, flow,
        vmem((2, micro, halo, chans), BF16),
        vmem((n_seq, micro, rows, LANES), BF16),
        vmem((n_seq, micro, rows, LANES), BF16),
        vmem((micro, n_seq * rows + 2 * EDGE, LANES), F32),
        vmem((n_seq, KERNEL * LANES, micro * rows), BF16),
        vmem((n_seq, micro, rows, chans), BF16),
        vmem((KERNEL * LANES, chans), F32),
        vmem((8, chans), F32),
        vmem((n_seq, 8, LANES), F32),
        vmem((n_seq, 8, LANES), F32),
        dma((2,)), dma((2,)), dma((2,)), dma((2,)),
        dma((micro, 2)), dma((micro, 2)), dma((micro, 2)), dma((micro, 2)),
        dma((n_seq,)), dma((n_seq,)), dma((n_seq,)), dma((n_seq,)),
        dma((n_seq, micro, 4)), dma((n_seq, micro)),
    ]
    conv_grad, gain_grad = pl.pallas_call(
        functools.partial(level_kernel, sections, n_seq, n_lo, micro, rows, chans, halo),
        out_shape=(
            jax.ShapeDtypeStruct((KERNEL, part, chans), BF16),
            jax.ShapeDtypeStruct((1, part), F32),
        ),
        in_specs=[pl.BlockSpec(memory_space=pltpu.VMEM)] * 5,
        out_specs=(pl.BlockSpec(memory_space=pltpu.VMEM),) * 2,
        scratch_shapes=scratch,
        compiler_params=pltpu.CompilerParams(
            collective_id=0, has_side_effects=True, vmem_limit_bytes=58 * 2**20
        ),
    )(spread, stem, conv_weight[0].reshape(KERNEL * chans, chans), block_gain, cotangent)
    return conv_grad[None], gain_grad


def solution(mesh):
    placed = (
        P(None, "seq"),
        P(),
        P("section", None, None, None),
        P("section", None),
        P(None, "seq", None),
    )
    return jax.shard_map(
        functools.partial(shards, mesh.shape["section"], mesh.shape["seq"]),
        mesh=mesh,
        in_specs=placed,
        out_specs=(P("section", None, "seq", None), P("section", "seq")),
        check_vma=False,
    )
```

time: 545 us -> 97.4 us (0.18)
  blocking collectives: 164 us -> 0 us
  waiting for transfers between devices: 135 us -> 0 us
  starting transfers between devices: 125 us -> 0 us
  Pallas kernels: 0 us -> 90.4 us
  other arithmetic: 46.1 us -> 1.43 us
  matrix products: 44.1 us -> 0 us
  between operations: 14.9 us -> 0.65 us
  local copies, waits for them, and re-layouts: 12.5 us -> 4.75 us
    all_to_all x6 -> x0, blocking collectives: 143 us -> none  [mirror(): lax.all_to_all(payload, 'section', split_axis=0, concat_axis=0, tiled=True)]
    ppermute x32 -> x0, starting transfers between devices: 105 us -> none  [the longest x11 60.3 us: padded_2(): before = lax.ppermute(last, axis, up)]
    pallas_call x0 -> x1, Pallas kernels: none -> 90.4 us  [shards(): pl.pallas_call(functools.partial(level_kernel, sections, n_seq, n_lo, mic...]
    reduce_scatter x1 -> x0, waiting for transfers between devices: 89.2 us -> none  [shards(): lax.psum_scatter(kernel_sum.astype(jnp.bfloat16), 'seq', scatter_dimensio...]
    dot_general x31 -> x0, matrix products: 44.1 us -> none  [the longest x10 19.3 us: backward_block(): jnp.einsum('rc,rd->cd', padded[offset:offset + row_count], grad_out, pref...]
    add x6 -> x0, other arithmetic: 28.4 us -> none  [the longest x4 27.8 us: backward_block(): return (kernel_sum + kernel_terms, gain_sum + grad_gain, grad_in)]
    ppermute x32 -> x0, waiting for transfers between devices: 25.7 us -> none  [the longest x11 10.5 us: padded_2(): before = lax.ppermute(last, axis, up)]
    unnamed x1 -> x0, blocking collectives: 21.3 us -> none
  transfers between devices with their start and end apart: 39 -> 0, of which waited for: 22 -> 0; matrix products, arithmetic and copies ran while one was open for 1% -> 0% of each run, Pallas kernels for 0% -> 0%
where the time goes in v1:
time: 97.4 us; the launch traced here: 97.2 us
  Pallas kernels  90.4 us (93%)
  local copies, waits for them, and re-layouts  4.75 us (5%)
  other arithmetic  1.43 us (1%)
    pallas_call x1, Pallas kernels, shards(): pl.pallas_call(functools.partial(level_kernel, sections, n_seq, n_lo, mic...  90.4 us
    unnamed x2, local copies, waits for them, and re-layouts  3.13 us

profile of v1, /device:TPU:0, one launch (start us, length us, event | category | flops | bytes accessed | tf_op | source)
XLA Modules:
  0.0 97.2 jit_solution(1758577134544977034)
XLA Ops:
  0.6 0.9 reshape.20
  1.6 0.7 pad.4.stem_ref
  2.3 1.4 %compare_convert_fusion.e_ref = f32[2,128,128]{2,1,0:T(8,128)} fusion(s32[128]{0:T(128)S(1)} %compare_select_fusion, s32[2,128]{1,0:T(2,128)} %param.5), kind=kLoop, calls=%fused_computation | loop fusion | flops 65536 | bytes 132608 | tf_op jit(solution)/shard_map/convert_element_type | solution.py:558
  3.7 90.4 %shard_map.68 = (bf16[5,96,768]{2,1,0:T(8,128)(2,1)}, f32[1,96]{1,0:T(1,128)}) custom-call(f32[2,128,128]{2,1,0:T(8,128)} %compare_convert_fusion.e_ref, bf16[128,768]{1,0:T(8,128)(2,1)} %pad.4.stem_ref, bf16[3840,768]{1,0:T(8,128)(2,1)} %bitcast.2, f32[1,768]{1,0:T(1,128)} %gain_ref.1, bf16[2,128,768]{2,1,0:T(8,128)(2,1)} %cot_ref.1), custom_call_target="tpu_custom_call" | custom-call | tf_op jit(solution)/shard_map/pallas_call | solution.py:585
  94.1 2.0 %copy.9 = bf16[1,5,96,768]{3,2,1,0:T(8,128)(2,1)} copy(bf16[1,5,96,768]{3,2,1,0:T(8,128)(2,1)} %bitcast.3) | data formatting | bytes 1474560
  96.1 1.1 %copy.10 = f32[1,96]{1,0:T(1,128)} copy(f32[1,96]{1,0:T(1,128)} %get-tuple-element.9) | data formatting | bytes 768
  (1 shorter events, 0.0 us)

commit v2 on v1

--- a/solution.py
+++ b/solution.py
@@ -29,12 +29,12 @@
 
 def level_kernel(
     sections, n_seq, n_lo, micro, rows, chans, halo,
-    e_ref, stem_ref, w_ref, gain_ref, cot_ref,
+    ids_ref, stem_ref, w_hbm, gain_ref, cot_ref,
     out_ref, gout_ref,
-    ebuf, bsum, actf, x5, gradf, gact, inflow, skip, fout, gin, gskip, gsend, coth,
+    w_ref, stemf, ebuf, bsum, actf, x5, gradf, gact, inflow, skip, fout, gin, gskip, gsend, coth,
     aslab, acol, acolf, a5t, gall, acc, gain_acc, gslab, grecv,
     e_send, e_recv, c_send, c_recv, f_send, f_recv, b_send, b_recv,
-    a_send, a_recv, n_send, n_recv, ag_send, ag_recv,
+    a_send, a_recv, n_send, n_recv, ag_send, ag_recv, w_sem,
 ):
     sec, q = lax.axis_index("section"), lax.axis_index("seq")
     n_hi = n_seq // n_lo
@@ -49,6 +49,8 @@
     step = 32
     tokens = rows * n_seq
 
+    w_copy = pltpu.make_async_copy(w_hbm, w_ref, w_sem)
+    w_copy.start()
     barrier = pltpu.get_barrier_semaphore()
     for d in range(1, n_seq):
         pl.semaphore_signal(
@@ -63,9 +65,9 @@
 
     def e_copy(side):
         if side == 0:
-            src, dst, to = e_ref.at[:, rows - e_halo : rows], ebuf.at[:, 0:e_halo], q + 1
+            src, dst, to = ebuf.at[:, rows : e_halo + rows], ebuf.at[:, 0:e_halo], q + 1
         else:
-            src, dst, to = e_ref.at[:, 0:e_halo], ebuf.at[:, e_halo + rows :], q - 1
+            src, dst, to = ebuf.at[:, e_halo : 2 * e_halo], ebuf.at[:, e_halo + rows :], q - 1
         return remote(src, dst, e_send.at[side], e_recv.at[side], seq=to)
 
     def c_copy(side):
@@ -102,9 +104,16 @@
     acolf[:, 0:EDGE] = jnp.zeros((micro, EDGE, LANES), F32)
     acolf[:, EDGE + tokens :] = jnp.zeros((micro, EDGE, LANES), F32)
     gain_acc[...] = jnp.zeros_like(gain_acc)
+    acc[...] = jnp.zeros_like(acc)
 
     @pl.when(sec == 0)
     def _():
+        lane = lax.broadcasted_iota(jnp.int32, (rows, LANES), 1)
+        wanted = jnp.where(lane < STEM_K * BASES, lane % BASES, -1).astype(F32)
+        for m in range(micro):
+            ids = jnp.broadcast_to(ids_ref[m : m + 1, :].astype(F32), (LANES, rows)).T
+            ebuf[m, e_halo : e_halo + rows] = jnp.where(ids == wanted, 1.0, 0.0)
+
         @pl.when(q < n_seq - 1)
         def _():
             e_copy(0).start()
@@ -113,7 +122,9 @@
         def _():
             e_copy(1).start()
 
-        ebuf[:, e_halo : e_halo + rows] = e_ref[...]
+        stemf[...] = jnp.zeros_like(stemf)
+        for k in range(STEM_K):
+            stemf[k * BASES : (k + 1) * BASES] = stem_ref[k].astype(F32)
 
         @pl.when(q == 0)
         def _():
@@ -158,6 +169,60 @@
 
         lax.fori_loop(0, chans // 256, tile, 0)
 
+    def multiply(block):
+        def tile(n, c):
+            at = pl.ds(pl.multiple_of(n * 256, 256), 256)
+            acc[:, at] += jnp.dot(
+                a5t[block], gall[block, :, :, at].reshape(micro * rows, 256),
+                preferred_element_type=F32,
+            )
+            return c
+
+        lax.fori_loop(0, chans // 256, tile, 0)
+
+    def gather(then):
+        then(q)
+        for d in range(1, n_hi):
+            for m in range(micro):
+                @pl.when(hi - d >= 0)
+                def _():
+                    gather_copy(q - d * n_lo, m, 0).wait_recv()
+                    each_way((0, 2, 3), q - d * n_lo, m, start)
+
+                @pl.when(hi + d < n_hi)
+                def _():
+                    gather_copy(q + d * n_lo, m, 1).wait_recv()
+                    each_way((1, 2, 3), q + d * n_lo, m, start)
+
+            @pl.when(hi - d >= 0)
+            def _():
+                then(q - d * n_lo)
+
+            @pl.when(hi + d < n_hi)
+            def _():
+                then(q + d * n_lo)
+
+        for e in range(1, n_lo):
+            for d in range(n_hi):
+                for side in (-1, 1) if d else (1,):
+                    h = hi + side * d
+
+                    @pl.when((h >= 0) & (h < n_hi) & (lo - e >= 0))
+                    def _():
+                        block = h * n_lo + lo - e
+                        for m in range(micro):
+                            gather_copy(block, m, 2).wait_recv()
+                            each_way((2,), block, m, start)
+                        then(block)
+
+                    @pl.when((h >= 0) & (h < n_hi) & (lo + e < n_lo))
+                    def _():
+                        block = h * n_lo + lo + e
+                        for m in range(micro):
+                            gather_copy(block, m, 3).wait_recv()
+                            each_way((3,), block, m, start)
+                        then(block)
+
     @pl.when(sec == last)
     def _():
         @pl.when(q < n_seq - 1)
@@ -191,11 +256,14 @@
             c_copy(1).wait_recv()
             gradf[:, EDGE + halo + rows : EDGE + ext] = coth[1].astype(F32)
 
+        w_copy.wait()
+
         def each(m, carry):
             conv_back(m)
             return carry
 
         lax.fori_loop(0, micro, each, 0)
+        gather(lambda block: None)
 
     def f_copy(m, kind):
         to = sec + 1 if kind == 0 else mirror_sec
@@ -222,7 +290,9 @@
             for k in range(STEM_K):
                 off = e_halo - halo + k - (STEM_K - 1) // 2
                 hot = jnp.where(tap == k, ebuf[m, off : off + ext], hot)
-            stem = jnp.dot(hot.astype(BF16), stem_ref[...], preferred_element_type=F32)
+            stem = jnp.dot(
+                hot.astype(BF16), stemf[...].astype(BF16), preferred_element_type=F32
+            )
             bsum[m] = stem.astype(BF16).astype(F32)
 
         @pl.when(sec > 0)
@@ -255,6 +325,10 @@
         @pl.when(sec < last)
         def _():
             shifted(actf, m, False)
+
+            @pl.when(m == 0)
+            def _():
+                w_copy.wait()
 
             def tile(n, c):
                 at = pl.ds(pl.multiple_of(n * 256, 256), 256)
@@ -394,19 +468,9 @@
 
     lax.fori_loop(0, micro, backward, 0)
 
-    for d in range(1, n_hi):
-        for m in range(micro):
-            @pl.when(hi - d >= 0)
-            def _():
-                block = q - d * n_lo
-                gather_copy(block, m, 0).wait_recv()
-                each_way((0, 2, 3), block, m, start)
-
-            @pl.when(hi + d < n_hi)
-            def _():
-                block = q + d * n_lo
-                gather_copy(block, m, 1).wait_recv()
-                each_way((1, 2, 3), block, m, start)
+    @pl.when((sec >= half) & (sec < last))
+    def _():
+        gather(lambda block: None)
 
     @pl.when(sec >= half)
     def _():
@@ -436,34 +500,18 @@
 
     lax.fori_loop(0, n_seq, gain_slab, 0)
 
-    for e in range(1, n_lo):
-        for h in range(n_hi):
-            for m in range(micro):
-                @pl.when(lo - e >= 0)
-                def _():
-                    block = h * n_lo + lo - e
-                    gather_copy(block, m, 2).wait_recv()
-                    each_way((2,), block, m, start)
-
-                @pl.when(lo + e < n_lo)
-                def _():
-                    block = h * n_lo + lo + e
-                    gather_copy(block, m, 3).wait_recv()
-                    each_way((3,), block, m, start)
-
-    acc[...] = jnp.zeros_like(acc)
-
-    def multiply(j, carry):
-        def tile(n, c):
-            at = pl.ds(pl.multiple_of(n * 256, 256), 256)
-            acc[:, at] += jnp.dot(
-                a5t[j], gall[j, :, :, at].reshape(micro * rows, 256), preferred_element_type=F32
-            )
-            return c
-
-        return lax.fori_loop(0, chans // 256, tile, carry)
-
-    lax.fori_loop(0, n_seq, multiply, 0)
+    @pl.when(sec < half)
+    def _():
+        gather(multiply)
+
+    @pl.when(sec >= half)
+    def _():
+        def one(j, carry):
+            multiply(j)
+            return carry
+
+        lax.fori_loop(0, n_seq, one, 0)
+
     for k in range(KERNEL):
         out_ref[k] = acc[k * LANES : k * LANES + part].astype(BF16)
 
@@ -543,6 +591,11 @@
         return carry
 
     lax.fori_loop(0, n_seq, sent, 0)
+
+
+def finish(conv_ref, gain_ref, out_ref, gout_ref):
+    out_ref[0] = conv_ref[...]
+    gout_ref[...] = gain_ref[...]
 
 
 def shards(sections, n_seq, base_ids, stem_weight, conv_weight, block_gain, cotangent):
@@ -552,14 +605,11 @@
     ext = rows + 2 * halo
     e_halo = halo + 16
     part = chans // n_seq
-    taps = STEM_K * BASES
-    lane = jnp.arange(LANES, dtype=jnp.int32)
-    wanted = jnp.where(lane < taps, lane % BASES, -1)
-    spread = (base_ids[:, :, None] == wanted).astype(F32)
-    stem = jnp.pad(stem_weight.reshape(taps, chans), ((0, LANES - taps), (0, 0)))
     vmem, dma = pltpu.VMEM, pltpu.SemaphoreType.DMA
     flow = vmem((micro, ext, chans), BF16)
     scratch = [
+        vmem((KERNEL * chans, chans), BF16),
+        vmem((LANES, chans), F32),
         vmem((micro, rows + 2 * e_halo, LANES), F32),
         vmem((micro, ext, chans), F32),
         vmem((micro, ext + 2 * EDGE, chans), F32),
@@ -580,7 +630,7 @@
         dma((2,)), dma((2,)), dma((2,)), dma((2,)),
         dma((micro, 2)), dma((micro, 2)), dma((micro, 2)), dma((micro, 2)),
         dma((n_seq,)), dma((n_seq,)), dma((n_seq,)), dma((n_seq,)),
-        dma((n_seq, micro, 4)), dma((n_seq, micro)),
+        dma((n_seq, micro, 4)), dma((n_seq, micro)), dma,
     ]
     conv_grad, gain_grad = pl.pallas_call(
         functools.partial(level_kernel, sections, n_seq, n_lo, micro, rows, chans, halo),
@@ -588,14 +638,24 @@
             jax.ShapeDtypeStruct((KERNEL, part, chans), BF16),
             jax.ShapeDtypeStruct((1, part), F32),
         ),
-        in_specs=[pl.BlockSpec(memory_space=pltpu.VMEM)] * 5,
+        in_specs=[pl.BlockSpec(memory_space=pl.ANY if i == 2 else vmem) for i in range(5)],
         out_specs=(pl.BlockSpec(memory_space=pltpu.VMEM),) * 2,
         scratch_shapes=scratch,
         compiler_params=pltpu.CompilerParams(
             collective_id=0, has_side_effects=True, vmem_limit_bytes=58 * 2**20
         ),
-    )(spread, stem, conv_weight[0].reshape(KERNEL * chans, chans), block_gain, cotangent)
-    return conv_grad[None], gain_grad
+    )(base_ids, stem_weight, conv_weight[0].reshape(KERNEL * chans, chans), block_gain, cotangent)
+    whole = pl.BlockSpec(memory_space=vmem)
+    conv_grad, gain_grad = pl.pallas_call(
+        finish,
+        out_shape=(
+            jax.ShapeDtypeStruct((1, KERNEL, part, chans), BF16),
+            jax.ShapeDtypeStruct((1, part), F32),
+        ),
+        in_specs=[whole, whole],
+        out_specs=(whole, whole),
+    )(conv_grad, gain_grad)
+    return conv_grad, gain_grad
 
 
 def solution(mesh):

time: 97.4 us -> 87.6 us (0.90)
  local copies, waits for them, and re-layouts: 4.75 us -> 0 us
  Pallas kernels: 90.4 us -> 86.8 us
  other arithmetic: 1.43 us -> 0 us
    pallas_call x1, Pallas kernels: 90.4 us -> 84.8 us  [shards(): pl.pallas_call(functools.partial(level_kernel, sections, n_seq, n_lo, mic...]
    unnamed x2 -> x0, local copies, waits for them, and re-layouts: 3.13 us -> none
    pallas_call x0 -> x1, Pallas kernels: none -> 2.03 us  [shards(): pl.pallas_call(finish, out_shape=(jax.ShapeDtypeStruct((1, KERNEL, part,...]
    convert_element_type x1 -> x0, other arithmetic: 1.42 us -> none  [shards(): spread = (base_ids[:, :, None] == wanted).astype(F32)]
where the time goes in v2:
time: 87.6 us; the launch traced here: 87.5 us
  Pallas kernels  86.8 us (99%)
    pallas_call x1, Pallas kernels, shards(): pl.pallas_call(functools.partial(level_kernel, sections, n_seq, n_lo, mic...  84.8 us
    pallas_call x1, Pallas kernels, shards(): pl.pallas_call(finish, out_shape=(jax.ShapeDtypeStruct((1, KERNEL, part,...  2.03 us

profile of v2, /device:TPU:0, one launch (start us, length us, event | category | flops | bytes accessed | tf_op | source)
XLA Modules:
  0.0 87.5 jit_solution(17553791930009779222)
XLA Ops:
  0.6 84.8 %shard_map.68 = (bf16[5,96,768]{2,1,0:T(8,128)(2,1)}, f32[1,96]{1,0:T(1,128)}) custom-call(s32[2,128]{1,0:T(2,128)} %ids_ref.1, bf16[15,4,768]{2,1,0:T(4,128)(2,1)} %stem_ref.1, bf16[3840,768]{1,0:T(8,128)(2,1)} %bitcast.1, f32[1,768]{1,0:T(1,128)} %gain_ref.1, bf16[2,128,768]{2,1,0:T(8,128)(2,1)} %cot_ref.1), custom_call_target="tpu_custom_call" | custom-call | tf_op jit(solution)/shard_map/pallas_call | solution.py:635
  85.4 2.0 %shard_map.69 = (bf16[1,5,96,768]{3,2,1,0:T(8,128)(2,1)}, f32[1,96]{1,0:T(1,128)}) custom-call(bf16[5,96,768]{2,1,0:T(8,128)(2,1)} %get-tuple-element.4.conv_ref, f32[1,96]{1,0:T(1,128)} %get-tuple-element.5.gain_ref), custom_call_target="tpu_custom_call" | custom-call | tf_op jit(solution)/shard_map/pallas_call | solution.py:649

commit v3 on v2

--- a/solution.py
+++ b/solution.py
@@ -180,7 +180,7 @@
 
         lax.fori_loop(0, chans // 256, tile, 0)
 
-    def gather(then):
+    def gather_column(then):
         then(q)
         for d in range(1, n_hi):
             for m in range(micro):
@@ -202,6 +202,7 @@
             def _():
                 then(q + d * n_lo)
 
+    def gather_row(then):
         for e in range(1, n_lo):
             for d in range(n_hi):
                 for side in (-1, 1) if d else (1,):
@@ -263,7 +264,7 @@
             return carry
 
         lax.fori_loop(0, micro, each, 0)
-        gather(lambda block: None)
+        gather_column(lambda block: None)
 
     def f_copy(m, kind):
         to = sec + 1 if kind == 0 else mirror_sec
@@ -280,160 +281,9 @@
             body(pl.multiple_of(i * step, step))
             return carry
 
-        lax.fori_loop(0, ext // step, one, 0)
-
-    def forward(m, carry):
-        @pl.when(sec == 0)
-        def _():
-            tap = lax.broadcasted_iota(jnp.int32, (ext, LANES), 1) // BASES
-            hot = jnp.zeros((ext, LANES), F32)
-            for k in range(STEM_K):
-                off = e_halo - halo + k - (STEM_K - 1) // 2
-                hot = jnp.where(tap == k, ebuf[m, off : off + ext], hot)
-            stem = jnp.dot(
-                hot.astype(BF16), stemf[...].astype(BF16), preferred_element_type=F32
-            )
-            bsum[m] = stem.astype(BF16).astype(F32)
-
-        @pl.when(sec > 0)
-        def _():
-            f_copy(m, 0).wait_recv()
-
-            @pl.when(sec < half)
-            def _():
-                bsum[m] = inflow[m].astype(F32)
-
-            @pl.when(sec == half)
-            def _():
-                bsum[m] = inflow[m].astype(F32) * 2.0
-
-            @pl.when(sec > half)
-            def _():
-                f_copy(m, 1).wait_recv()
-                bsum[m] = inflow[m].astype(F32) + skip[m].astype(F32)
-
-        def act_rows(r):
-            b = bsum[m, pl.ds(r, step)]
-            scale = lax.rsqrt(jnp.mean(b * b, axis=-1, keepdims=True) + 1e-06)
-            x = b * scale * gain_ref[...]
-            t = jnp.tanh(GELU_A * (x + GELU_B * (x * x * x)))
-            y = (x * (0.5 * (1.0 + t))).astype(BF16).astype(F32)
-            actf[m, pl.ds(pl.multiple_of(EDGE + r, 8), step)] = jnp.where(row_mask(r, step), y, 0.0)
-
-        by_rows(act_rows)
-
-        @pl.when(sec < last)
-        def _():
-            shifted(actf, m, False)
-
-            @pl.when(m == 0)
-            def _():
-                w_copy.wait()
-
-            def tile(n, c):
-                at = pl.ds(pl.multiple_of(n * 256, 256), 256)
-                total = bsum[m, :, at] + jnp.dot(
-                    x5[...], w_ref[:, at], preferred_element_type=F32
-                )
-                fout[m, :, at] = total.astype(BF16)
-                return c
-
-            lax.fori_loop(0, chans // 256, tile, 0)
-            f_copy(m, 0).start()
-
-            @pl.when(sec < half - 1)
-            def _():
-                f_copy(m, 1).start()
-
-        return carry
-
-    lax.fori_loop(0, micro, forward, 0)
-
-    def picker(j):
-        c = lax.broadcasted_iota(jnp.int32, (chans, LANES), 0)
-        lane = lax.broadcasted_iota(jnp.int32, (chans, LANES), 1)
-        return jnp.where((c == j * part + lane) & (lane < part), 1.0, 0.0).astype(BF16)
-
-    def a_copy(j):
-        return remote(aslab.at[j], acol.at[q], a_send.at[j], a_recv.at[q], seq=j)
-
-    def a_from(j):
-        return remote(aslab.at[j], acol.at[j], a_send.at[j], a_recv.at[j], seq=j)
-
-    def spread_rows():
-        own = slice(EDGE + halo, EDGE + halo + rows)
-
-        def slab(j, carry):
-            pick = picker(j)
-            for m in range(micro):
-                aslab[j, m] = jnp.dot(
-                    actf[m, own].astype(BF16), pick, preferred_element_type=F32
-                ).astype(BF16)
-
-            @pl.when(j != q)
-            def _():
-                a_copy(j).start()
-
-            @pl.when(j == q)
-            def _():
-                acol[j] = aslab[j]
-
-            return carry
-
-        lax.fori_loop(0, n_seq, slab, 0)
-
-        def take(j, carry):
-            @pl.when(j != q)
-            def _():
-                a_from(j).wait_recv()
-
-            at = pl.ds(pl.multiple_of(EDGE + j * rows, 8), rows)
-            for m in range(micro):
-                acolf[m, at] = acol[j, m].astype(F32)
-            return carry
-
-        lax.fori_loop(0, n_seq, take, 0)
-
-        def turn(j, carry):
-            for m in range(micro):
-                window = acolf[m, pl.ds(pl.multiple_of(j * rows, rows), rows + 2 * EDGE)]
-                for k in range(KERNEL):
-                    off = EDGE + k - reach
-                    a5t[j, k * LANES : (k + 1) * LANES, m * rows : (m + 1) * rows] = (
-                        window[off : off + rows].T.astype(BF16)
-                    )
-            return carry
-
-        lax.fori_loop(0, n_seq, turn, 0)
-
-    @pl.when(sec < half)
-    def _():
-        spread_rows()
-
-    def backward(m, carry):
-        @pl.when(sec < last)
-        def _():
-            b_copy(m, 0).wait_recv()
-
-            @pl.when(sec < half - 1)
-            def _():
-                b_copy(m, 1).wait_recv()
-                gradf[m, EDGE : EDGE + ext] = (
-                    (gin[m].astype(F32) + gskip[m].astype(F32)).astype(BF16).astype(F32)
-                )
-
-            @pl.when(sec == half - 1)
-            def _():
-                gradf[m, EDGE : EDGE + ext] = gin[m].astype(F32) * 2.0
-
-            @pl.when(sec >= half)
-            def _():
-                gradf[m, EDGE : EDGE + ext] = gin[m].astype(F32)
-
-            gall[q, m] = gradf[m, EDGE + halo : EDGE + halo + rows].astype(BF16)
-            each_way(range(4), q, m, start)
-            conv_back(m)
-
+        lax.fori_loop(0, ext // step, one, 0, unroll=True)
+
+    def pull_back(m):
         def pull_rows(r):
             at = pl.ds(r, step)
             b, grad = bsum[m, at], gact[m, at]
@@ -464,13 +314,175 @@
             def _():
                 b_copy(m, 1).start()
 
+
+    def forward(m, carry):
+        @pl.when(sec == 0)
+        def _():
+            tap = lax.broadcasted_iota(jnp.int32, (ext, LANES), 1) // BASES
+            hot = jnp.zeros((ext, LANES), F32)
+            for k in range(STEM_K):
+                off = e_halo - halo + k - (STEM_K - 1) // 2
+                hot = jnp.where(tap == k, ebuf[m, off : off + ext], hot)
+            stem = jnp.dot(
+                hot.astype(BF16), stemf[...].astype(BF16), preferred_element_type=F32
+            )
+            bsum[m] = stem.astype(BF16).astype(F32)
+
+        @pl.when(sec > 0)
+        def _():
+            f_copy(m, 0).wait_recv()
+
+            @pl.when(sec < half)
+            def _():
+                bsum[m] = inflow[m].astype(F32)
+
+            @pl.when(sec == half)
+            def _():
+                bsum[m] = inflow[m].astype(F32) * 2.0
+
+            @pl.when(sec > half)
+            def _():
+                f_copy(m, 1).wait_recv()
+                bsum[m] = inflow[m].astype(F32) + skip[m].astype(F32)
+
+        @pl.when(sec == last)
+        def _():
+            pull_back(m)
+
+        def act_rows(r):
+            b = bsum[m, pl.ds(r, step)]
+            scale = lax.rsqrt(jnp.mean(b * b, axis=-1, keepdims=True) + 1e-06)
+            x = b * scale * gain_ref[...]
+            t = jnp.tanh(GELU_A * (x + GELU_B * (x * x * x)))
+            y = (x * (0.5 * (1.0 + t))).astype(BF16).astype(F32)
+            actf[m, pl.ds(pl.multiple_of(EDGE + r, 8), step)] = jnp.where(row_mask(r, step), y, 0.0)
+
+        by_rows(act_rows)
+
+        @pl.when(sec < last)
+        def _():
+            shifted(actf, m, False)
+
+            @pl.when(m == 0)
+            def _():
+                w_copy.wait()
+
+            def tile(n, c):
+                at = pl.ds(pl.multiple_of(n * 256, 256), 256)
+                total = bsum[m, :, at] + jnp.dot(
+                    x5[...], w_ref[:, at], preferred_element_type=F32
+                )
+                fout[m, :, at] = total.astype(BF16)
+                return c
+
+            lax.fori_loop(0, chans // 256, tile, 0)
+            f_copy(m, 0).start()
+
+            @pl.when(sec < half - 1)
+            def _():
+                f_copy(m, 1).start()
+
         return carry
 
-    lax.fori_loop(0, micro, backward, 0)
+    lax.fori_loop(0, micro, forward, 0)
+
+    def picker(j):
+        c = lax.broadcasted_iota(jnp.int32, (chans, LANES), 0)
+        lane = lax.broadcasted_iota(jnp.int32, (chans, LANES), 1)
+        return jnp.where((c == j * part + lane) & (lane < part), 1.0, 0.0).astype(BF16)
+
+    def a_copy(j):
+        return remote(aslab.at[j], acol.at[q], a_send.at[j], a_recv.at[q], seq=j)
+
+    def a_from(j):
+        return remote(aslab.at[j], acol.at[j], a_send.at[j], a_recv.at[j], seq=j)
+
+    def spread_rows():
+        own = slice(EDGE + halo, EDGE + halo + rows)
+
+        def slab(j, carry):
+            pick = picker(j)
+            for m in range(micro):
+                aslab[j, m] = jnp.dot(
+                    actf[m, own].astype(BF16), pick, preferred_element_type=F32
+                ).astype(BF16)
+
+            @pl.when(j != q)
+            def _():
+                a_copy(j).start()
+
+            @pl.when(j == q)
+            def _():
+                acol[j] = aslab[j]
+
+            return carry
+
+        lax.fori_loop(0, n_seq, slab, 0)
+
+        def take(j, carry):
+            @pl.when(j != q)
+            def _():
+                a_from(j).wait_recv()
+
+            at = pl.ds(pl.multiple_of(EDGE + j * rows, 8), rows)
+            for m in range(micro):
+                acolf[m, at] = acol[j, m].astype(F32)
+            return carry
+
+        lax.fori_loop(0, n_seq, take, 0)
+
+        def turn(j, carry):
+            for m in range(micro):
+                window = acolf[m, pl.ds(pl.multiple_of(j * rows, rows), rows + 2 * EDGE)]
+                for k in range(KERNEL):
+                    off = EDGE + k - reach
+                    a5t[j, k * LANES : (k + 1) * LANES, m * rows : (m + 1) * rows] = (
+                        window[off : off + rows].T.astype(BF16)
+                    )
+            return carry
+
+        lax.fori_loop(0, n_seq, turn, 0)
+
+    @pl.when(sec < half)
+    def _():
+        spread_rows()
+
+    def backward(m, carry):
+        b_copy(m, 0).wait_recv()
+
+        @pl.when(sec < half - 1)
+        def _():
+            b_copy(m, 1).wait_recv()
+            gradf[m, EDGE : EDGE + ext] = (
+                (gin[m].astype(F32) + gskip[m].astype(F32)).astype(BF16).astype(F32)
+            )
+
+        @pl.when(sec == half - 1)
+        def _():
+            gradf[m, EDGE : EDGE + ext] = gin[m].astype(F32) * 2.0
+
+        @pl.when(sec >= half)
+        def _():
+            gradf[m, EDGE : EDGE + ext] = gin[m].astype(F32)
+
+        gall[q, m] = gradf[m, EDGE + halo : EDGE + halo + rows].astype(BF16)
+        each_way(range(4), q, m, start)
+        conv_back(m)
+
+        pull_back(m)
+        return carry
+
+    @pl.when(sec < last)
+    def _():
+        lax.fori_loop(0, micro, backward, 0)
 
     @pl.when((sec >= half) & (sec < last))
     def _():
-        gather(lambda block: None)
+        gather_column(lambda block: None)
+
+    @pl.when(sec >= half)
+    def _():
+        gather_row(lambda block: None)
 
     @pl.when(sec >= half)
     def _():
@@ -502,7 +514,8 @@
 
     @pl.when(sec < half)
     def _():
-        gather(multiply)
+        gather_column(multiply)
+        gather_row(multiply)
 
     @pl.when(sec >= half)
     def _():

time: 87.6 us -> 81 us (0.925)
  Pallas kernels: 86.8 us -> 80.2 us
    pallas_call x1, Pallas kernels: 84.8 us -> 78.2 us  [shards(): pl.pallas_call(functools.partial(level_kernel, sections, n_seq, n_lo, mic...]
where the time goes in v3:
time: 81 us; the launch traced here: 80.9 us
  Pallas kernels  80.2 us (99%)
    pallas_call x1, Pallas kernels, shards(): pl.pallas_call(functools.partial(level_kernel, sections, n_seq, n_lo, mic...  78.2 us
    pallas_call x1, Pallas kernels, shards(): pl.pallas_call(finish, out_shape=(jax.ShapeDtypeStruct((1, KERNEL, part,...  2.03 us

profile of v3, /device:TPU:0, one launch (start us, length us, event | category | flops | bytes accessed | tf_op | source)
XLA Modules:
  0.0 80.9 jit_solution(7317716792161998165)
XLA Ops:
  0.6 78.2 %shard_map.68 = (bf16[5,96,768]{2,1,0:T(8,128)(2,1)}, f32[1,96]{1,0:T(1,128)}) custom-call(s32[2,128]{1,0:T(2,128)} %ids_ref.1, bf16[15,4,768]{2,1,0:T(4,128)(2,1)} %stem_ref.1, bf16[3840,768]{1,0:T(8,128)(2,1)} %bitcast.1, f32[1,768]{1,0:T(1,128)} %gain_ref.1, bf16[2,128,768]{2,1,0:T(8,128)(2,1)} %cot_ref.1), custom_call_target="tpu_custom_call" | custom-call | tf_op jit(solution)/shard_map/pallas_call | solution.py:648
  78.8 2.0 %shard_map.69 = (bf16[1,5,96,768]{3,2,1,0:T(8,128)(2,1)}, f32[1,96]{1,0:T(1,128)}) custom-call(bf16[5,96,768]{2,1,0:T(8,128)(2,1)} %get-tuple-element.4.conv_ref, f32[1,96]{1,0:T(1,128)} %get-tuple-element.5.gain_ref), custom_call_target="tpu_custom_call" | custom-call | tf_op jit(solution)/shard_map/pallas_call | solution.py:662

commit v4 on v3

--- a/solution.py
+++ b/solution.py
@@ -13,6 +13,7 @@
 LANES = 128
 EDGE = 8
 F32, BF16 = jnp.float32, jnp.bfloat16
+FULL, MAIN, SIDE = 0, 1, 2
 GELU_A, GELU_B = 0.7978845608028654, 0.044715
 
 
@@ -35,6 +36,7 @@
     aslab, acol, acolf, a5t, gall, acc, gain_acc, gslab, grecv,
     e_send, e_recv, c_send, c_recv, f_send, f_recv, b_send, b_recv,
     a_send, a_recv, n_send, n_recv, ag_send, ag_recv, w_sem,
+    rbuf, r_send, r_recv, u_send, u_recv, d_send, d_recv,
 ):
     sec, q = lax.axis_index("section"), lax.axis_index("seq")
     n_hi = n_seq // n_lo
@@ -44,6 +46,7 @@
     e_halo = halo + 16
     part = chans // n_seq
     reach = (KERNEL - 1) // 2
+    cut = chans * 2 // 3 // LANES * LANES
     last = sections - 1
     mirror_sec = last - sec
     step = 32
@@ -77,20 +80,33 @@
             src, dst, to = cot_ref.at[:, 0:halo], coth.at[1], q - 1
         return remote(src, dst, c_send.at[side], c_recv.at[side], seq=to)
 
-    def gather_copy(block, m, way):
+    def gather_copy(kind, block, m, way):
         to = [q + n_lo, q - n_lo, q + 1, q - 1][way]
+        if kind == SIDE:
+            here, sends, lands = rbuf.at[block, m], r_send, r_recv
+        else:
+            here = gall.at[block, m] if kind == FULL else gall.at[block, m, :, 0:cut]
+            sends, lands = ag_send, ag_recv
+        return remote(here, here, sends.at[block, m, way], lands.at[block, m], seq=to)
+
+    def raise_copy(m):
         return remote(
-            gall.at[block, m], gall.at[block, m], ag_send.at[block, m, way],
-            ag_recv.at[block, m], seq=to,
+            gall.at[q, m, :, cut:], rbuf.at[q, m], u_send.at[m], u_recv.at[m], section=sec + half
         )
 
+    def lower_copy(block, m, to):
+        return remote(
+            rbuf.at[block, m], gall.at[block, m, :, cut:], d_send.at[block, m],
+            d_recv.at[block, m], section=to,
+        )
+
     up, down, right, left = hi < n_hi - 1, hi > 0, lo < n_lo - 1, lo > 0
 
-    def each_way(ways, block, m, act):
+    def each_way(kind, ways, block, m, act):
         for way in ways:
             @pl.when([up, down, right, left][way])
             def _():
-                act(gather_copy(block, m, way))
+                act(gather_copy(kind, block, m, way))
 
     def start(copy):
         copy.start()
@@ -180,29 +196,17 @@
 
         lax.fori_loop(0, chans // 256, tile, 0)
 
-    def gather_column(then):
-        then(q)
+    def column_blocks(body):
         for d in range(1, n_hi):
-            for m in range(micro):
-                @pl.when(hi - d >= 0)
-                def _():
-                    gather_copy(q - d * n_lo, m, 0).wait_recv()
-                    each_way((0, 2, 3), q - d * n_lo, m, start)
-
-                @pl.when(hi + d < n_hi)
-                def _():
-                    gather_copy(q + d * n_lo, m, 1).wait_recv()
-                    each_way((1, 2, 3), q + d * n_lo, m, start)
-
             @pl.when(hi - d >= 0)
             def _():
-                then(q - d * n_lo)
+                body(q - d * n_lo, 0, (0, 2, 3))
 
             @pl.when(hi + d < n_hi)
             def _():
-                then(q + d * n_lo)
-
-    def gather_row(then):
+                body(q + d * n_lo, 1, (1, 2, 3))
+
+    def row_blocks(body):
         for e in range(1, n_lo):
             for d in range(n_hi):
                 for side in (-1, 1) if d else (1,):
@@ -210,19 +214,47 @@
 
                     @pl.when((h >= 0) & (h < n_hi) & (lo - e >= 0))
                     def _():
-                        block = h * n_lo + lo - e
-                        for m in range(micro):
-                            gather_copy(block, m, 2).wait_recv()
-                            each_way((2,), block, m, start)
-                        then(block)
+                        body(h * n_lo + lo - e, 2, (2,))
 
                     @pl.when((h >= 0) & (h < n_hi) & (lo + e < n_lo))
                     def _():
-                        block = h * n_lo + lo + e
-                        for m in range(micro):
-                            gather_copy(block, m, 3).wait_recv()
-                            each_way((3,), block, m, start)
-                        then(block)
+                        body(h * n_lo + lo + e, 3, (3,))
+
+    def taking(kind, then=None):
+        def body(block, way, onward):
+            for m in range(micro):
+                gather_copy(kind, block, m, way).wait_recv()
+                each_way(kind, onward, block, m, start)
+                if kind == SIDE:
+                    lower_copy(block, m, sec - half).start()
+            if then is not None:
+                then(block)
+
+        return body
+
+    def joined(block, way=0, onward=()):
+        for m in range(micro):
+            lower_copy(block, m, sec + half).wait_recv()
+        multiply(block)
+
+    def relay():
+        for m in range(micro):
+            raise_copy(m).wait_recv()
+            each_way(SIDE, range(4), q, m, start)
+        column_blocks(taking(SIDE))
+        row_blocks(taking(SIDE))
+
+    def drained(kind):
+        def body(block, way, onward):
+            for m in range(micro):
+                each_way(kind, onward, block, m, wait_send)
+                if kind == SIDE:
+                    lower_copy(block, m, sec - half).wait_send()
+
+        for m in range(micro):
+            each_way(kind, range(4), q, m, wait_send)
+        column_blocks(body)
+        row_blocks(body)
 
     @pl.when(sec == last)
     def _():
@@ -236,7 +268,7 @@
 
         gall[q] = cot_ref[...]
         for m in range(micro):
-            each_way(range(4), q, m, start)
+            each_way(FULL, range(4), q, m, start)
         gradf[:, EDGE + halo : EDGE + halo + rows] = cot_ref[...].astype(F32)
 
         @pl.when(q == 0)
@@ -264,7 +296,7 @@
             return carry
 
         lax.fori_loop(0, micro, each, 0)
-        gather_column(lambda block: None)
+        column_blocks(taking(FULL))
 
     def f_copy(m, kind):
         to = sec + 1 if kind == 0 else mirror_sec
@@ -431,13 +463,21 @@
 
         lax.fori_loop(0, n_seq, take, 0)
 
+        eye = jnp.where(
+            lax.broadcasted_iota(jnp.int32, (LANES, LANES), 0)
+            == lax.broadcasted_iota(jnp.int32, (LANES, LANES), 1), 1.0, 0.0,
+        ).astype(BF16)
+
         def turn(j, carry):
             for m in range(micro):
                 window = acolf[m, pl.ds(pl.multiple_of(j * rows, rows), rows + 2 * EDGE)]
                 for k in range(KERNEL):
                     off = EDGE + k - reach
                     a5t[j, k * LANES : (k + 1) * LANES, m * rows : (m + 1) * rows] = (
-                        window[off : off + rows].T.astype(BF16)
+                        lax.dot_general(
+                            eye, window[off : off + rows].astype(BF16),
+                            (((1,), (1,)), ((), ())), preferred_element_type=F32,
+                        ).astype(BF16)
                     )
             return carry
 
@@ -466,9 +506,17 @@
             gradf[m, EDGE : EDGE + ext] = gin[m].astype(F32)
 
         gall[q, m] = gradf[m, EDGE + halo : EDGE + halo + rows].astype(BF16)
-        each_way(range(4), q, m, start)
+
+        @pl.when(sec < half)
+        def _():
+            each_way(MAIN, range(4), q, m, start)
+            raise_copy(m).start()
+
+        @pl.when(sec >= half)
+        def _():
+            each_way(FULL, range(4), q, m, start)
+
         conv_back(m)
-
         pull_back(m)
         return carry
 
@@ -476,17 +524,15 @@
     def _():
         lax.fori_loop(0, micro, backward, 0)
 
-    @pl.when((sec >= half) & (sec < last))
-    def _():
-        gather_column(lambda block: None)
-
     @pl.when(sec >= half)
     def _():
-        gather_row(lambda block: None)
-
-    @pl.when(sec >= half)
-    def _():
         spread_rows()
+
+        @pl.when(sec < last)
+        def _():
+            column_blocks(taking(FULL, multiply))
+
+        relay()
 
     def n_copy(j):
         return remote(gslab.at[j], grecv.at[q], n_send.at[j], n_recv.at[q], seq=j)
@@ -512,18 +558,21 @@
 
     lax.fori_loop(0, n_seq, gain_slab, 0)
 
+    multiply(q)
+
     @pl.when(sec < half)
     def _():
-        gather_column(multiply)
-        gather_row(multiply)
+        column_blocks(taking(MAIN))
+        column_blocks(joined)
+        row_blocks(taking(MAIN, joined))
 
     @pl.when(sec >= half)
     def _():
-        def one(j, carry):
-            multiply(j)
-            return carry
-
-        lax.fori_loop(0, n_seq, one, 0)
+        @pl.when(sec == last)
+        def _():
+            column_blocks(lambda block, way, onward: multiply(block))
+
+        row_blocks(taking(FULL, multiply))
 
     for k in range(KERNEL):
         out_ref[k] = acc[k * LANES : k * LANES + part].astype(BF16)
@@ -575,25 +624,18 @@
         def _():
             b_copy(m, 1).wait_send()
 
-        each_way(range(4), q, m, wait_send)
-        for d in range(1, n_hi):
-            @pl.when(hi - d >= 0)
-            def _():
-                each_way((0, 2, 3), q - d * n_lo, m, wait_send)
-
-            @pl.when(hi + d < n_hi)
-            def _():
-                each_way((1, 2, 3), q + d * n_lo, m, wait_send)
-
-        for e in range(1, n_lo):
-            for h in range(n_hi):
-                @pl.when(lo - e >= 0)
-                def _():
-                    each_way((2,), h * n_lo + lo - e, m, wait_send)
-
-                @pl.when(lo + e < n_lo)
-                def _():
-                    each_way((3,), h * n_lo + lo + e, m, wait_send)
+        @pl.when(sec < half)
+        def _():
+            raise_copy(m).wait_send()
+
+    @pl.when(sec < half)
+    def _():
+        drained(MAIN)
+
+    @pl.when(sec >= half)
+    def _():
+        drained(FULL)
+        drained(SIDE)
 
     def sent(j, carry):
         @pl.when(j != q)
@@ -644,6 +686,9 @@
         dma((micro, 2)), dma((micro, 2)), dma((micro, 2)), dma((micro, 2)),
         dma((n_seq,)), dma((n_seq,)), dma((n_seq,)), dma((n_seq,)),
         dma((n_seq, micro, 4)), dma((n_seq, micro)), dma,
+        vmem((n_seq, micro, rows, chans - chans * 2 // 3 // LANES * LANES), BF16),
+        dma((n_seq, micro, 4)), dma((n_seq, micro)), dma((micro,)), dma((micro,)),
+        dma((n_seq, micro)), dma((n_seq, micro)),
     ]
     conv_grad, gain_grad = pl.pallas_call(
         functools.partial(level_kernel, sections, n_seq, n_lo, micro, rows, chans, halo),

time: 81 us -> 88.3 us (1.090)
  Pallas kernels: 80.2 us -> 87.5 us
    pallas_call x1, Pallas kernels: 78.2 us -> 85.5 us  [shards(): pl.pallas_call(functools.partial(level_kernel, sections, n_seq, n_lo, mic...]
where the time goes in v4:
time: 88.3 us; the launch traced here: 88.2 us
  Pallas kernels  87.5 us (99%)
    pallas_call x1, Pallas kernels, shards(): pl.pallas_call(functools.partial(level_kernel, sections, n_seq, n_lo, mic...  85.5 us
    pallas_call x1, Pallas kernels, shards(): pl.pallas_call(finish, out_shape=(jax.ShapeDtypeStruct((1, KERNEL, part,...  2.03 us

profile of v4, /device:TPU:0, one launch (start us, length us, event | category | flops | bytes accessed | tf_op | source)
XLA Modules:
  0.0 88.2 jit_solution(7379545576695651691)
XLA Ops:
  0.6 85.5 %shard_map.68 = (bf16[5,96,768]{2,1,0:T(8,128)(2,1)}, f32[1,96]{1,0:T(1,128)}) custom-call(s32[2,128]{1,0:T(2,128)} %ids_ref.1, bf16[15,4,768]{2,1,0:T(4,128)(2,1)} %stem_ref.1, bf16[3840,768]{1,0:T(8,128)(2,1)} %bitcast.1, f32[1,768]{1,0:T(1,128)} %gain_ref.1, bf16[2,128,768]{2,1,0:T(8,128)(2,1)} %cot_ref.1), custom_call_target="tpu_custom_call" | custom-call | tf_op jit(solution)/shard_map/pallas_call | solution.py:693
  86.1 2.0 %shard_map.69 = (bf16[1,5,96,768]{3,2,1,0:T(8,128)(2,1)}, f32[1,96]{1,0:T(1,128)}) custom-call(bf16[5,96,768]{2,1,0:T(8,128)(2,1)} %get-tuple-element.4.conv_ref, f32[1,96]{1,0:T(1,128)} %get-tuple-element.5.gain_ref), custom_call_target="tpu_custom_call" | custom-call | tf_op jit(solution)/shard_map/pallas_call | solution.py:707

commit v5 on v4

--- a/solution.py
+++ b/solution.py
@@ -13,7 +13,7 @@
 LANES = 128
 EDGE = 8
 F32, BF16 = jnp.float32, jnp.bfloat16
-FULL, MAIN, SIDE = 0, 1, 2
+FULL, MAIN, SIDE, FIRST = 0, 1, 2, 3
 GELU_A, GELU_B = 0.7978845608028654, 0.044715
 
 
@@ -82,22 +82,26 @@
 
     def gather_copy(kind, block, m, way):
         to = [q + n_lo, q - n_lo, q + 1, q - 1][way]
-        if kind == SIDE:
-            here, sends, lands = rbuf.at[block, m], r_send, r_recv
+        if kind >= SIDE:
+            slot = kind - SIDE
+            here, sends, lands = rbuf.at[slot, block, m], r_send.at[slot], r_recv.at[slot]
         else:
             here = gall.at[block, m] if kind == FULL else gall.at[block, m, :, 0:cut]
             sends, lands = ag_send, ag_recv
         return remote(here, here, sends.at[block, m, way], lands.at[block, m], seq=to)
 
-    def raise_copy(m):
+    def raise_copy(kind, m):
+        slot = kind - SIDE
         return remote(
-            gall.at[q, m, :, cut:], rbuf.at[q, m], u_send.at[m], u_recv.at[m], section=sec + half
+            gall.at[q, m, :, cut:], rbuf.at[slot, q, m], u_send.at[m], u_recv.at[slot, m],
+            section=last if kind == FIRST else sec + half,
         )
 
-    def lower_copy(block, m, to):
+    def lower_copy(kind, block, m):
+        slot = kind - SIDE
         return remote(
-            rbuf.at[block, m], gall.at[block, m, :, cut:], d_send.at[block, m],
-            d_recv.at[block, m], section=to,
+            rbuf.at[slot, block, m], gall.at[block, m, :, cut:], d_send.at[slot, block, m],
+            d_recv.at[block, m], section=0 if kind == FIRST else sec - half,
         )
 
     up, down, right, left = hi < n_hi - 1, hi > 0, lo < n_lo - 1, lo > 0
@@ -196,8 +200,8 @@
 
         lax.fori_loop(0, chans // 256, tile, 0)
 
-    def column_blocks(body):
-        for d in range(1, n_hi):
+    def column_blocks(body, distances=range(1, n_hi)):
+        for d in distances:
             @pl.when(hi - d >= 0)
             def _():
                 body(q - d * n_lo, 0, (0, 2, 3))
@@ -225,8 +229,8 @@
             for m in range(micro):
                 gather_copy(kind, block, m, way).wait_recv()
                 each_way(kind, onward, block, m, start)
-                if kind == SIDE:
-                    lower_copy(block, m, sec - half).start()
+                if kind >= SIDE:
+                    lower_copy(kind, block, m).start()
             if then is not None:
                 then(block)
 
@@ -234,22 +238,34 @@
 
     def joined(block, way=0, onward=()):
         for m in range(micro):
-            lower_copy(block, m, sec + half).wait_recv()
+            remote(
+                rbuf.at[0, block, m], gall.at[block, m, :, cut:], d_send.at[0, block, m],
+                d_recv.at[block, m], section=last,
+            ).wait_recv()
         multiply(block)
 
-    def relay():
-        for m in range(micro):
-            raise_copy(m).wait_recv()
-            each_way(SIDE, range(4), q, m, start)
-        column_blocks(taking(SIDE))
-        row_blocks(taking(SIDE))
+    def relay(kinds):
+        def stage(kind, at):
+            if at == 0:
+                for m in range(micro):
+                    raise_copy(kind, m).wait_recv()
+                    each_way(kind, range(4), q, m, start)
+            elif at < n_hi:
+                column_blocks(taking(kind), (at,))
+            elif at == n_hi:
+                row_blocks(taking(kind))
+
+        for at in range(n_hi + len(kinds)):
+            for lag, kind in enumerate(kinds):
+                if at >= lag:
+                    stage(kind, at - lag)
 
     def drained(kind):
         def body(block, way, onward):
             for m in range(micro):
                 each_way(kind, onward, block, m, wait_send)
-                if kind == SIDE:
-                    lower_copy(block, m, sec - half).wait_send()
+                if kind >= SIDE:
+                    lower_copy(kind, block, m).wait_send()
 
         for m in range(micro):
             each_way(kind, range(4), q, m, wait_send)
@@ -510,7 +526,14 @@
         @pl.when(sec < half)
         def _():
             each_way(MAIN, range(4), q, m, start)
-            raise_copy(m).start()
+
+            @pl.when(sec > 0)
+            def _():
+                raise_copy(SIDE, m).start()
+
+            @pl.when(sec == 0)
+            def _():
+                raise_copy(FIRST, m).start()
 
         @pl.when(sec >= half)
         def _():
@@ -526,13 +549,20 @@
 
     @pl.when(sec >= half)
     def _():
+        @pl.when(sec < last)
+        def _():
+            column_blocks(taking(FULL))
+
         spread_rows()
 
-        @pl.when(sec < last)
-        def _():
-            column_blocks(taking(FULL, multiply))
-
-        relay()
+        if last > half + 1:
+            @pl.when((sec > half) & (sec < last))
+            def _():
+                relay((SIDE,))
+
+        @pl.when(sec == last)
+        def _():
+            relay((SIDE, FIRST))
 
     def n_copy(j):
         return remote(gslab.at[j], grecv.at[q], n_send.at[j], n_recv.at[q], seq=j)
@@ -568,10 +598,7 @@
 
     @pl.when(sec >= half)
     def _():
-        @pl.when(sec == last)
-        def _():
-            column_blocks(lambda block, way, onward: multiply(block))
-
+        column_blocks(lambda block, way, onward: multiply(block))
         row_blocks(taking(FULL, multiply))
 
     for k in range(KERNEL):
@@ -626,7 +653,7 @@
 
         @pl.when(sec < half)
         def _():
-            raise_copy(m).wait_send()
+            raise_copy(SIDE, m).wait_send()
 
     @pl.when(sec < half)
     def _():
@@ -635,7 +662,14 @@
     @pl.when(sec >= half)
     def _():
         drained(FULL)
-        drained(SIDE)
+
+        @pl.when(sec > half)
+        def _():
+            drained(SIDE)
+
+        @pl.when(sec == last)
+        def _():
+            drained(FIRST)
 
     def sent(j, carry):
         @pl.when(j != q)
@@ -686,9 +720,9 @@
         dma((micro, 2)), dma((micro, 2)), dma((micro, 2)), dma((micro, 2)),
         dma((n_seq,)), dma((n_seq,)), dma((n_seq,)), dma((n_seq,)),
         dma((n_seq, micro, 4)), dma((n_seq, micro)), dma,
-        vmem((n_seq, micro, rows, chans - chans * 2 // 3 // LANES * LANES), BF16),
-        dma((n_seq, micro, 4)), dma((n_seq, micro)), dma((micro,)), dma((micro,)),
-        dma((n_seq, micro)), dma((n_seq, micro)),
+        vmem((2, n_seq, micro, rows, chans - chans * 2 // 3 // LANES * LANES), BF16),
+        dma((2, n_seq, micro, 4)), dma((2, n_seq, micro)), dma((micro,)), dma((2, micro)),
+        dma((2, n_seq, micro)), dma((n_seq, micro)),
     ]
     conv_grad, gain_grad = pl.pallas_call(
         functools.partial(level_kernel, sections, n_seq, n_lo, micro, rows, chans, halo),

time: 88.3 us -> 83.7 us (0.948)
  Pallas kernels: 87.5 us -> 82.5 us
    pallas_call x1, Pallas kernels: 85.5 us -> 80.4 us  [shards(): pl.pallas_call(functools.partial(level_kernel, sections, n_seq, n_lo, mic...]
where the time goes in v5:
time: 83.7 us; the launch traced here: 83.1 us
  Pallas kernels  82.5 us (99%)
    pallas_call x1, Pallas kernels, shards(): pl.pallas_call(functools.partial(level_kernel, sections, n_seq, n_lo, mic...  80.4 us
    pallas_call x1, Pallas kernels, shards(): pl.pallas_call(finish, out_shape=(jax.ShapeDtypeStruct((1, KERNEL, part,...  2.03 us

profile of v5, /device:TPU:0, one launch (start us, length us, event | category | flops | bytes accessed | tf_op | source)
XLA Modules:
  0.0 83.1 jit_solution(7990094309652118050)
XLA Ops:
  0.6 80.4 %shard_map.68 = (bf16[5,96,768]{2,1,0:T(8,128)(2,1)}, f32[1,96]{1,0:T(1,128)}) custom-call(s32[2,128]{1,0:T(2,128)} %ids_ref.1, bf16[15,4,768]{2,1,0:T(4,128)(2,1)} %stem_ref.1, bf16[3840,768]{1,0:T(8,128)(2,1)} %bitcast.1, f32[1,768]{1,0:T(1,128)} %gain_ref.1, bf16[2,128,768]{2,1,0:T(8,128)(2,1)} %cot_ref.1), custom_call_target="tpu_custom_call" | custom-call | tf_op jit(solution)/shard_map/pallas_call | solution.py:727
  81.1 2.0 %shard_map.69 = (bf16[1,5,96,768]{3,2,1,0:T(8,128)(2,1)}, f32[1,96]{1,0:T(1,128)}) custom-call(bf16[5,96,768]{2,1,0:T(8,128)(2,1)} %get-tuple-element.4.conv_ref, f32[1,96]{1,0:T(1,128)} %get-tuple-element.5.gain_ref), custom_call_target="tpu_custom_call" | custom-call | tf_op jit(solution)/shard_map/pallas_call | solution.py:741

commit v6 on v5

--- a/solution.py
+++ b/solution.py
@@ -40,6 +40,7 @@
 ):
     sec, q = lax.axis_index("section"), lax.axis_index("seq")
     n_hi = n_seq // n_lo
+    shared = (sec > 0) & (sec < sections // 2)
     hi, lo = q // n_lo, q % n_lo
     half = sections // 2
     ext = rows + 2 * halo
@@ -523,19 +524,12 @@
 
         gall[q, m] = gradf[m, EDGE + halo : EDGE + halo + rows].astype(BF16)
 
-        @pl.when(sec < half)
+        @pl.when(shared)
         def _():
             each_way(MAIN, range(4), q, m, start)
-
-            @pl.when(sec > 0)
-            def _():
-                raise_copy(SIDE, m).start()
-
-            @pl.when(sec == 0)
-            def _():
-                raise_copy(FIRST, m).start()
-
-        @pl.when(sec >= half)
+            raise_copy(SIDE, m).start()
+
+        @pl.when(jnp.logical_not(shared))
         def _():
             each_way(FULL, range(4), q, m, start)
 
@@ -555,14 +549,9 @@
 
         spread_rows()
 
-        if last > half + 1:
-            @pl.when((sec > half) & (sec < last))
-            def _():
-                relay((SIDE,))
-
-        @pl.when(sec == last)
-        def _():
-            relay((SIDE, FIRST))
+        @pl.when(sec > half)
+        def _():
+            relay((SIDE,))
 
     def n_copy(j):
         return remote(gslab.at[j], grecv.at[q], n_send.at[j], n_recv.at[q], seq=j)
@@ -590,7 +579,13 @@
 
     multiply(q)
 
-    @pl.when(sec < half)
+    @pl.when(sec == 0)
+    def _():
+        column_blocks(taking(FULL))
+        column_blocks(lambda block, way, onward: multiply(block))
+        row_blocks(taking(FULL, multiply))
+
+    @pl.when(shared)
     def _():
         column_blocks(taking(MAIN))
         column_blocks(joined)
@@ -651,25 +646,21 @@
         def _():
             b_copy(m, 1).wait_send()
 
-        @pl.when(sec < half)
+        @pl.when(shared)
         def _():
             raise_copy(SIDE, m).wait_send()
 
-    @pl.when(sec < half)
+    @pl.when(shared)
     def _():
         drained(MAIN)
 
-    @pl.when(sec >= half)
+    @pl.when(jnp.logical_not(shared))
     def _():
         drained(FULL)
 
-        @pl.when(sec > half)
-        def _():
-            drained(SIDE)
-
-        @pl.when(sec == last)
-        def _():
-            drained(FIRST)
+    @pl.when(sec > half)
+    def _():
+        drained(SIDE)
 
     def sent(j, carry):
         @pl.when(j != q)

time: 83.7 us -> 79.6 us (0.951)
  Pallas kernels: 82.5 us -> 78.2 us
    pallas_call x1, Pallas kernels: 80.4 us -> 76.2 us  [shards(): pl.pallas_call(functools.partial(level_kernel, sections, n_seq, n_lo, mic...]
where the time goes in v6:
time: 79.6 us; the launch traced here: 78.8 us
  Pallas kernels  78.2 us (98%)
    pallas_call x1, Pallas kernels, shards(): pl.pallas_call(functools.partial(level_kernel, sections, n_seq, n_lo, mic...  76.2 us
    pallas_call x1, Pallas kernels, shards(): pl.pallas_call(finish, out_shape=(jax.ShapeDtypeStruct((1, KERNEL, part,...  2.03 us

profile of v6, /device:TPU:0, one launch (start us, length us, event | category | flops | bytes accessed | tf_op | source)
XLA Modules:
  0.0 78.8 jit_solution(12420898202310827620)
XLA Ops:
  0.6 76.2 %shard_map.68 = (bf16[5,96,768]{2,1,0:T(8,128)(2,1)}, f32[1,96]{1,0:T(1,128)}) custom-call(s32[2,128]{1,0:T(2,128)} %ids_ref.1, bf16[15,4,768]{2,1,0:T(4,128)(2,1)} %stem_ref.1, bf16[3840,768]{1,0:T(8,128)(2,1)} %bitcast.1, f32[1,768]{1,0:T(1,128)} %gain_ref.1, bf16[2,128,768]{2,1,0:T(8,128)(2,1)} %cot_ref.1), custom_call_target="tpu_custom_call" | custom-call | tf_op jit(solution)/shard_map/pallas_call | solution.py:718
  76.8 2.0 %shard_map.69 = (bf16[1,5,96,768]{3,2,1,0:T(8,128)(2,1)}, f32[1,96]{1,0:T(1,128)}) custom-call(bf16[5,96,768]{2,1,0:T(8,128)(2,1)} %get-tuple-element.4.conv_ref, f32[1,96]{1,0:T(1,128)} %get-tuple-element.5.gain_ref), custom_call_target="tpu_custom_call" | custom-call | tf_op jit(solution)/shard_map/pallas_call | solution.py:732
